TPU v7x, 32 devices: a whole 2x2x4 slice. The times are simulated.
32 devices in a mesh: gx: 4 (over z), gy: 8 (over y, x, core).
Axes of the slice: x: 2, y: 2, z: 4, core: 2. Of those that a mesh axis runs over, the one named last changes fastest.
Arguments:
- seismic: float32 [512, 512, 256], P('gx', 'gy'), may hold values from -41 to 41, as said below
Outputs:
- shift_field: float32 [512, 512, 256], P('gx', 'gy')
- residual: float32 [512, 512, 256], P('gx', 'gy')
Inputs may be any that keep to these rules, and one draw needn't show every extreme that they name: `seismic`: recorded amplitudes of the window.
All inputs are finite; a program needn't handle non-finite values.
Results may differ from a plain program's by a relative error of at most 0.0003.
Values sent between devices are 32-bit elements; how exact they have to be, the bound alone decides.
A program may use at most 320 MiB of HBM per device.

v0:
```python
import jax
import jax.numpy as jnp
from jax import lax
from jax.sharding import PartitionSpec as P

NX = 512
NY = 512
ITERS = 2


damping = 0.001
floor_term = 0.5
highest = lax.Precision.HIGHEST


def extended(block, sides, width):
    for axis, dim in sides:
        count = lax.axis_size(axis)
        forward = [(i, i + 1) for i in range(count - 1)]
        backward = [(target, source) for source, target in forward]
        low = lax.ppermute(
            lax.slice_in_dim(block, block.shape[dim] - width, None, axis=dim), axis, forward
        )
        high = lax.ppermute(lax.slice_in_dim(block, 0, width, axis=dim), axis, backward)
        block = jnp.concatenate([low, block, high], axis=dim)
    return block


def cut(field, start, stop, axis):
    return lax.slice_in_dim(field, start, stop, axis=axis)


def smooth_axis(field, axis):
    length = field.shape[axis]
    return 0.25 * (
        cut(field, 0, length - 2, axis)
        + 2.0 * cut(field, 1, length - 1, axis)
        + cut(field, 2, length, axis)
    )


def pad_time(field):
    return jnp.pad(field, ((0, 0), (0, 0), (1, 1)))


def smooth_all(field):
    return smooth_axis(pad_time(smooth_axis(smooth_axis(field, 0), 1)), 2)


def tensor_fields(padded, inside_x, inside_y):
    mask = inside_x[:, None, None] * inside_y[None, :, None]
    grad_x = 0.5 * (padded[2:, 1:-1] - padded[:-2, 1:-1]) * mask
    grad_y = 0.5 * (padded[1:-1, 2:] - padded[1:-1, :-2]) * mask
    timed = pad_time(padded[1:-1, 1:-1])
    grad_t = 0.5 * (timed[:, :, 2:] - timed[:, :, :-2]) * mask
    cross_x = smooth_all(grad_x * grad_t)
    cross_y = smooth_all(grad_y * grad_t)
    along_t = smooth_all(grad_t * grad_t) + floor_term
    spread = smooth_all(grad_x * grad_x + grad_y * grad_y)
    return (-cross_x / along_t, -cross_y / along_t, along_t / (along_t + spread))


def cosine_table(order):
    freq = jnp.arange(order, dtype=jnp.float32)[:, None]
    place = jnp.arange(order, dtype=jnp.float32)[None, :]
    scale = jnp.where(freq == 0.0, jnp.sqrt(1.0 / order), jnp.sqrt(2.0 / order)).astype(jnp.float32)
    return scale * jnp.cos(jnp.pi * (place + 0.5) * freq / order)


def eigen_values(order):
    freq = jnp.arange(order, dtype=jnp.float32)
    return 2.0 - 2.0 * jnp.cos(jnp.pi * freq / order)


def combine_terms(field, upper_x, lower_x, upper_y, lower_y, weight_x, weight_y, prior_x, prior_y):
    return (
        damping * field
        + weight_x * (field - upper_x)
        + prior_x * (field - lower_x)
        + weight_y * (field - upper_y)
        + prior_y * (field - lower_y)
    )


def operate(field, weight_x, weight_y, prior_x, prior_y):
    padded = extended(field, (("gx", 0), ("gy", 1)), 1)
    return combine_terms(
        field,
        padded[2:, 1:-1],
        padded[:-2, 1:-1],
        padded[1:-1, 2:],
        padded[1:-1, :-2],
        weight_x,
        weight_y,
        prior_x,
        prior_y,
    )


def solve_front(front, table_x, table_y, plane_denom):
    hat = jnp.einsum("ki,tij->tkj", table_x, front, precision=highest)
    hat = jnp.einsum("lj,tkj->tkl", table_y, hat, precision=highest)
    hat = hat / plane_denom
    hat = jnp.einsum("lj,tkl->tkj", table_y, hat, precision=highest)
    return jnp.einsum("ki,tkj->tij", table_x, hat, precision=highest)


def slice_solve(whole, table_x, table_y, plane_denom):
    front = jnp.transpose(whole, (2, 0, 1))
    return jnp.transpose(solve_front(front, table_x, table_y, plane_denom), (1, 2, 0))


def reorder_back(back, rows_x, rows_y, parts_x, parts_y, depth):
    per = depth // (parts_x * parts_y)
    target = jnp.arange(depth, dtype=jnp.int32)
    outer = target // (parts_y * per)
    middle = target // per % parts_y
    source = middle * (parts_x * per) + outer * per + target % per
    select = (jnp.arange(depth, dtype=jnp.int32)[:, None] == source[None, :]).astype(jnp.float32)
    flat = back.reshape(rows_x * rows_y, depth)
    return jnp.dot(flat, select, precision=highest, preferred_element_type=jnp.float32).reshape(
        rows_x, rows_y, depth
    )


def inner(first, second):
    return lax.psum(jnp.sum(first * second), ("gx", "gy"))


def solve(rhs, apply_op, precondition):
    shift_field = jnp.zeros_like(rhs)
    residual = rhs
    precond = precondition(residual)
    direction = precond
    norm_now = inner(residual, precond)
    for step in range(ITERS):
        image = apply_op(direction)
        alpha = norm_now / lax.psum(jnp.sum(direction * image), ("gx", "gy"))
        shift_field = shift_field + alpha * direction
        residual = residual - alpha * image
        if step + 1 < ITERS:
            precond = precondition(residual)
            norm_next = inner(residual, precond)
            direction = precond + norm_next / norm_now * direction
            norm_now = norm_next
    return (shift_field, residual)


def per_device(seismic):
    rows_x, rows_y, depth = seismic.shape
    parts_x = lax.axis_size("gx")
    parts_y = lax.axis_size("gy")
    base_x = lax.axis_index("gx") * rows_x
    base_y = lax.axis_index("gy") * rows_y
    table_x = cosine_table(NX)
    table_y = cosine_table(NY)
    eigen_x = eigen_values(NX)
    eigen_y = eigen_values(NY)
    plane_denom = damping + eigen_x[:, None] + eigen_y[None, :]
    padded = extended(seismic, (("gx", 0), ("gy", 1)), 3)
    grid_x = base_x + jnp.arange(-2, rows_x + 2, dtype=jnp.int32)
    grid_y = base_y + jnp.arange(-2, rows_y + 2, dtype=jnp.int32)
    inside_x = ((grid_x >= 0) & (grid_x < NX)).astype(jnp.float32)
    inside_y = ((grid_y >= 0) & (grid_y < NY)).astype(jnp.float32)
    dip_x, dip_y, weight = tensor_fields(padded, inside_x, inside_y)
    edge_x = grid_x[1:-1]
    edge_y = grid_y[1:-1]
    keep_x = ((edge_x >= 0) & (edge_x < NX - 1)).astype(jnp.float32)
    keep_y = ((edge_y >= 0) & (edge_y < NY - 1)).astype(jnp.float32)
    weight_x = weight * keep_x[:, None, None]
    weight_y = weight * keep_y[None, :, None]
    flux_x = weight_x * dip_x
    flux_y = weight_y * dip_y
    rhs = flux_x[:-2, 1:-1] - flux_x[1:-1, 1:-1] + (flux_y[1:-1, :-2] - flux_y[1:-1, 1:-1])
    own_x = weight_x[1:-1, 1:-1]
    prior_x = weight_x[:-2, 1:-1]
    own_y = weight_y[1:-1, 1:-1]
    prior_y = weight_y[1:-1, :-2]

    def precondition(field):
        whole = lax.all_to_all(
            lax.all_to_all(field, "gx", split_axis=2, concat_axis=0, tiled=True),
            "gy",
            split_axis=2,
            concat_axis=1,
            tiled=True,
        )
        hat = slice_solve(whole, table_x, table_y, plane_denom)
        back = lax.all_to_all(
            lax.all_to_all(hat, "gx", split_axis=0, concat_axis=2, tiled=True),
            "gy",
            split_axis=1,
            concat_axis=2,
            tiled=True,
        )
        return reorder_back(back, rows_x, rows_y, parts_x, parts_y, depth)

    def apply_tiles(field):
        return operate(field, own_x, own_y, prior_x, prior_y)

    return solve(rhs, apply_tiles, precondition)


def solution(mesh):
    placed = (P("gx", "gy", None),)
    return jax.shard_map(
        per_device,
        mesh=mesh,
        in_specs=placed,
        out_specs=(P("gx", "gy", None), P("gx", "gy", None)),
        check_vma=False,
    )
```

profile of v0, /device:TPU:0, one launch (start us, length us, event | category | flops | bytes accessed | tf_op | source)
XLA Modules:
  0.0 2077.2 jit_solution(1720866723027973175)
XLA Ops:
  0.6 8.2 copy.195
  12.4 4.9 collective-permute-start
  18.8 4.1 collective-permute-done
  22.8 4.1 collective-permute-done.1
  34.8 3.8 pad_maximum_fusion
  42.4 4.6 slice.298
  47.0 54.0 %fusion.77 = (f32[132,68,256]{2,0,1:T(8,128)}, f32[132,68,256]{2,0,1:T(8,128)}, f32[132,68,256]{2,0,1:T(8,128)}, f32[132,68,256]{2,0,1:T(8,128)}) fusion(f32[132,68]{0,1:T(8,128)S(1)} %multiply_multiply_fusion, f32[134,70,256]{2,0,1:T(8,128)} %copy-done.2, f32[132,68,256]{2,0,1:T(8,128)} %slice.298), kind=kLoop, calls=%fused_computation.146 | loop fusion | flops 36765696 | bytes 82758720 | tf_op jit(solution)/shard_map/mul | solution.py:57
  101.0 29.4 %fusion.6 = (f32[130,68,256]{2,0,1:T(8,128)}, f32[130,68,256]{2,0,1:T(8,128)}) fusion(f32[132,68,256]{2,0,1:T(8,128)} %get-tuple-element.29, f32[132,68,256]{2,0,1:T(8,128)} %get-tuple-element.30), kind=kLoop, calls=%fused_computation.23 | loop fusion | flops 18104320 | bytes 72417280 | tf_op jit(solution)/shard_map/mul | solution.py:35
  130.3 13.7 broadcast_multiply_fusion.4
  145.2 5.0 broadcast_multiply_fusion.5
  150.2 29.4 %fusion.2 = (f32[130,68,256]{2,0,1:T(8,128)}, f32[130,68,256]{2,0,1:T(8,128)}) fusion(f32[132,68,256]{2,0,1:T(8,128)} %get-tuple-element.27, f32[132,68,256]{2,0,1:T(8,128)} %get-tuple-element.28), kind=kLoop, calls=%fused_computation.15 | loop fusion | flops 18104320 | bytes 72417280 | tf_op jit(solution)/shard_map/mul | solution.py:35
  179.6 13.8 broadcast_multiply_fusion.3
  194.5 5.4 broadcast_multiply_fusion.2
  203.3 45.0 %fusion.24 = (f32[130,66,256]{2,0,1:T(8,128)}, f32[130,66,256]{2,0,1:T(8,128)}, f32[130,66,256]{2,0,1:T(8,128)}, f32[130,66,256]{2,0,1:T(8,128)}) fusion(f32[130,66,256]{2,0,1:T(8,128)} %broadcast_multiply_fusion.3, f32[130,68,256]{2,0,1:T(8,128)} %get-tuple-element.46, f32[130]{0:T(256)S(1)} %and_convert_fusion.1, f32[130,68,256]{2,0,1:T(8,128)S(1)} %bitcast.93, ...), kind=kLoop, calls=%fused_computation.47 | loop fusion | flops 61501440 | bytes 140575232 | tf_op jit(solution)/shard_map/mul | solution.py:172
  248.3 26.7 %fusion.30 = (f32[130,66,256]{2,0,1:T(8,128)}, f32[130,66,256]{2,0,1:T(8,128)}) fusion(f32[130,66,256]{2,0,1:T(8,128)} %get-tuple-element.24, f32[130,66,256]{2,0,1:T(8,128)} %broadcast_multiply_fusion.2, f32[130,68,256]{2,0,1:T(8,128)} %get-tuple-element.45, f32[130,66,256]{2,0,1:T(8,128)} %get-tuple-element.23, f32[66]{0:T(128)S(1)} %copy-done.9), kind=kLoop, calls=%fused_computation.53 | loop fusion | flops 24161280 | bytes 70287624 | tf_op jit(solution)/shard_map/mul | solution.py:173
  275.0 16.4 fusion.59
  291.3 8.7 copy.198
  300.0 185.5 %all_to_all.138 = f32[128,64,256]{0,1,2:T(8,128)S(1)} all-to-all(f32[128,64,256]{0,1,2:T(8,128)} %copy.198), channel_id=1, replica_groups=mesh['gx'=4,'gy'=8] {'gx'}, dimensions={2} | all-to-all | bytes 16777216 | tf_op jit(solution)/shard_map/all_to_all | solution.py:182
  485.5 4.5 copy.275
  490.0 11.4 all-to-all-start.1
  501.6 94.0 %all-to-all-done.1 = f32[512,64,64]{0,1,2:T(8,128)} async-done(((f32[512,64,64]{0,1,2:T(8,128)}), f32[512,64,64]{0,1,2:T(8,128)}, u32[]{:S(2)}, u32[]{:S(2)}) %all-to-all-start.1) | async-done | bytes 8388640 | tf_op jit(solution)/shard_map/all_to_all | solution.py:181
  595.6 8.1 copy.203
  603.7 22.6 %fusion.66 = f32[8,512,512]{2,1,0:T(8,128)S(1)} fusion(f32[512,512,8]{0,2,1:T(8,128)S(1)} %bitcast.102, f32[512]{0:T(512)S(1)} %get-tuple-element.49, f32[512]{0:T(512)S(1)} %get-tuple-element.50), kind=kOutput, calls=%fused_computation.117 | convolution fusion | flops 12885688320 | bytes 16781312 | tf_op jit(solution)/shard_map/ki,tij->tkj/dot_general | solution.py:101
  626.3 34.1 %fusion.64 = f32[8,512,512]{2,1,0:T(8,128)S(1)} fusion(f32[8,512,512]{2,1,0:T(8,128)S(1)} %fusion.66, f32[512]{0:T(512)S(1)} %get-tuple-element.49, f32[512]{0:T(512)S(1)} %get-tuple-element.50), kind=kOutput, calls=%fused_computation.115 | convolution fusion | flops 12885688320 | bytes 16781312 | tf_op jit(solution)/shard_map/lj,tkj->tkl/dot_general | solution.py:102
  660.4 19.8 fusion.72
  680.2 23.2 %convolution_bitcast_fusion.1 = f32[512,512,8]{0,1,2:T(8,128)} fusion(f32[8,512,512]{1,2,0:T(8,128)S(1)} %fusion.72, f32[512]{0:T(512)S(1)} %get-tuple-element.49, f32[512]{0:T(512)S(1)} %get-tuple-element.50), kind=kOutput, calls=%fused_computation.144 | convolution fusion | flops 12885688320 | bytes 16781312 | tf_op jit(solution)/shard_map/ki,tkj->tij/dot_general | solution.py:105
  703.4 10.5 copy.207
  713.9 184.9 %all_to_all.139 = f32[512,512,8]{1,2,0:T(8,128)S(1)} all-to-all(f32[512,512,8]{1,2,0:T(8,128)} %copy.207), channel_id=1, replica_groups=mesh['gx'=4,'gy'=8] {'gx'}, dimensions={0} | all-to-all | bytes 16777216 | tf_op jit(solution)/shard_map/all_to_all | solution.py:190
  898.8 4.4 copy.277
  903.2 11.0 copy.209
  914.3 5.0 all-to-all-start.3
  919.2 94.1 %all-to-all-done.3 = f32[128,512,32]{0,2,1:T(8,128)} async-done(((f32[128,512,32]{0,2,1:T(8,128)}), f32[128,512,32]{0,2,1:T(8,128)}, u32[]{:S(2)}, u32[]{:S(2)}) %all-to-all-start.3) | async-done | bytes 8388640 | tf_op jit(solution)/shard_map/all_to_all | solution.py:189
  1013.3 12.3 copy.210
  1025.6 14.7 reshape.169
  1040.3 9.4 fusion.111
  1051.0 5.0 collective-permute-start.5
  1056.0 4.9 copy.211
  1069.4 36.8 %multiply_reduce_fusion.2 = (f32[]{:T(128)}, f32[]{:T(128)}, f32[128,64,256]{2,0,1:T(8,128)}) fusion(f32[128,64,256]{2,1,0:T(8,128)} %bitcast.97, f32[128,64,256]{2,0,1:T(8,128)} %fusion.59, f32[128,64,256]{2,0,1:T(8,128)} %copy-done.7, f32[1,64,256]{2,0,1:T(1,128)S(1)} %copy.214, f32[1,64,256]{2,0,1:T(1,128)S(1)} %copy.216, ...), kind=kLoop, calls=%fused_computation.131 | loop fusion | flops 52428800 | bytes 67506184 | tf_op jit(solution)/shard_map/reduce_sum | solution.py:138
  1106.2 41.2 %all-reduce.5 = (f32[]{:T(128)}, f32[]{:T(128)}) all-reduce(f32[]{:T(128)} %get-tuple-element.15, f32[]{:T(128)} %get-tuple-element.14), channel_id=1, replica_groups=mesh['gx'=4,'gy'=8] {'gx','gy'}, use_global_device_ids=true, to_apply=%region_1.2 | all-reduce | flops 2 | bytes 16 | tf_op jit(solution)/shard_map/psum | solution.py:127
  1148.7 11.6 multiply_subtract_fusion.1
  1160.3 8.7 copy.226
  1169.1 186.9 %all_to_all.140 = f32[128,64,256]{0,1,2:T(8,128)S(1)} all-to-all(f32[128,64,256]{0,1,2:T(8,128)} %copy.226), channel_id=1, replica_groups=mesh['gx'=4,'gy'=8] {'gx'}, dimensions={2} | all-to-all | bytes 16777216 | tf_op jit(solution)/shard_map/all_to_all | solution.py:182
  1357.0 97.9 %all_to_all.141 = f32[512,64,64]{0,1,2:T(8,128)} all-to-all(f32[512,64,64]{0,1,2:T(8,128)S(1)} %bitcast.109), channel_id=1, replica_groups=mesh['gx'=4,'gy'=8] {'gy'}, dimensions={2} | all-to-all | bytes 16777216 | tf_op jit(solution)/shard_map/all_to_all | solution.py:181
  1455.0 8.1 copy.231
  1463.1 22.6 %fusion.62 = f32[8,512,512]{2,1,0:T(8,128)S(1)} fusion(f32[512,512,8]{0,2,1:T(8,128)S(1)} %bitcast.103, f32[512]{0:T(512)S(1)} %get-tuple-element.49, f32[512]{0:T(512)S(1)} %get-tuple-element.50), kind=kOutput, calls=%fused_computation.113 | convolution fusion | flops 12885688320 | bytes 16781312 | tf_op jit(solution)/shard_map/ki,tij->tkj/dot_general | solution.py:101
  1485.7 34.1 %fusion.60 = f32[8,512,512]{2,1,0:T(8,128)S(1)} fusion(f32[8,512,512]{2,1,0:T(8,128)S(1)} %fusion.62, f32[512]{0:T(512)S(1)} %get-tuple-element.49, f32[512]{0:T(512)S(1)} %get-tuple-element.50), kind=kOutput, calls=%fused_computation.111 | convolution fusion | flops 12885688320 | bytes 16781312 | tf_op jit(solution)/shard_map/lj,tkj->tkl/dot_general | solution.py:102
  1519.8 19.8 fusion.70
  1539.6 23.2 %convolution_bitcast_fusion = f32[512,512,8]{0,1,2:T(8,128)} fusion(f32[8,512,512]{1,2,0:T(8,128)S(1)} %fusion.70, f32[512]{0:T(512)S(1)} %get-tuple-element.49, f32[512]{0:T(512)S(1)} %get-tuple-element.50), kind=kOutput, calls=%fused_computation.143 | convolution fusion | flops 12885688320 | bytes 16781312 | tf_op jit(solution)/shard_map/ki,tkj->tij/dot_general | solution.py:105
  1562.8 10.4 copy.235
  1573.3 187.0 %all_to_all.142 = f32[512,512,8]{1,2,0:T(8,128)S(1)} all-to-all(f32[512,512,8]{1,2,0:T(8,128)} %copy.235), channel_id=1, replica_groups=mesh['gx'=4,'gy'=8] {'gx'}, dimensions={0} | all-to-all | bytes 16777216 | tf_op jit(solution)/shard_map/all_to_all | solution.py:190
  1760.2 4.3 copy.276
  1764.5 11.0 copy.237
  1775.5 97.8 %all_to_all.143 = f32[128,512,32]{0,2,1:T(8,128)S(1)} all-to-all(f32[128,512,32]{0,2,1:T(8,128)} %copy.237), channel_id=1, replica_groups=mesh['gx'=4,'gy'=8] {'gy'}, dimensions={1} | all-to-all | bytes 16777216 | tf_op jit(solution)/shard_map/all_to_all | solution.py:189
  1873.3 5.3 copy.238
  1879.8 14.6 multiply_reduce_fusion.1
  1894.3 38.5 %psum.30 = f32[]{:T(128)} all-reduce(f32[]{:T(128)} %get-tuple-element.43), channel_id=1, replica_groups=mesh['gx'=4,'gy'=8] {'gx','gy'}, use_global_device_ids=true, to_apply=%region_5.6 | all-reduce | flops 1 | bytes 8 | tf_op jit(solution)/shard_map/psum | solution.py:127
  1934.2 14.2 multiply_add_fusion.2
  1951.3 4.5 collective-permute-start.9
  1964.1 20.2 multiply_reduce_fusion
  1984.3 45.3 %psum.31 = f32[]{:T(128)} all-reduce(f32[]{:T(128)} %get-tuple-element.18), channel_id=1, replica_groups=mesh['gx'=4,'gy'=8] {'gx','gy'}, use_global_device_ids=true, to_apply=%region_7.8 | all-reduce | flops 1 | bytes 8 | tf_op jit(solution)/shard_map/psum | solution.py:138
  2030.9 14.2 multiply_add_fusion.1
  2045.1 11.6 multiply_subtract_fusion
  2056.7 12.0 copy.242
  2068.7 8.3 copy.241
  (78 shorter events, 45.6 us)
Async XLA Ops:
  8.9 3.4 copy-start.5
  12.4 10.5 collective-permute-start
  17.3 9.7 collective-permute-start.1
  18.7 16.2 copy-start.6
  28.2 3.8 collective-permute-start.2
  29.5 5.4 collective-permute-start.3
  38.7 3.7 copy-start.2
  130.3 14.9 copy-start
  179.6 14.9 copy-start.1
  179.6 20.3 slice-start
  179.6 20.3 slice-start.1
  179.6 21.7 %slice-start.3 = ((s8[9469952]{0:T(1024)(128)(4,1)}), s8[4194304]{0:T(1024)(128)(4,1)S(1)}, s32[]{:S(2)}) async-start(s8[9469952]{0:T(1024)(128)(4,1)} %bitcast.94), calls=%async_computation.11 | async-start | bytes 8388608
  179.6 22.9 %slice-start.4 = ((s8[9469952]{0:T(1024)(128)(4,1)}), s8[4194304]{0:T(1024)(128)(4,1)S(1)}, s32[]{:S(2)}) async-start(s8[9469952]{0:T(1024)(128)(4,1)} %bitcast.94), calls=%async_computation.12 | async-start | bytes 8388608
  194.5 8.5 slice-start.2
  194.5 8.8 slice-start.5
  203.3 45.0 %copy-start.9 = (f32[66]{0:T(128)S(1)}, f32[66]{0:T(128)}, u32[]{:S(2)}) copy-start(f32[66]{0:T(128)} %and_convert_fusion) | copy-start | bytes 796
  490.0 105.6 %all-to-all-start.1 = ((f32[512,64,64]{0,1,2:T(8,128)}), f32[512,64,64]{0,1,2:T(8,128)}, u32[]{:S(2)}, u32[]{:S(2)}) async-start(f32[512,64,64]{0,1,2:T(8,128)} %bitcast.104), calls=%async_computation.1 | async-start | bytes 16777216 | tf_op jit(solution)/shard_map/all_to_all | solution.py:181
  914.3 99.0 %all-to-all-start.3 = ((f32[128,512,32]{0,2,1:T(8,128)}), f32[128,512,32]{0,2,1:T(8,128)}, u32[]{:S(2)}, u32[]{:S(2)}) async-start(f32[128,512,32]{0,2,1:T(8,128)} %copy.209), calls=%async_computation.3 | async-start | bytes 16777216 | tf_op jit(solution)/shard_map/all_to_all | solution.py:189
  1049.7 11.4 copy-start.3
  1049.7 11.1 collective-permute-start.4
  1051.0 9.9 collective-permute-start.5
  1060.9 3.3 copy-start.7
  1064.1 4.3 collective-permute-start.6
  1065.4 4.0 collective-permute-start.7
  1873.3 5.3 slice-start.6
  1873.3 6.5 slice-start.7
  1948.3 15.8 copy-start.4
  1949.8 6.4 collective-permute-start.8
  1951.3 6.4 collective-permute-start.9
  1958.8 4.3 collective-permute-start.10
  1960.1 4.0 collective-permute-start.11
  2056.7 12.0 copy-start.8
where the time goes:
time: 2080 us
  blocking collectives  1060 us (51%)
  other arithmetic  354 us (17%)
  matrix products  223 us (11%)
  waiting for transfers between devices  203 us (10%)
  local copies, waits for them, and re-layouts  180 us (9%)
  starting transfers between devices  46.8 us (2%)
    all_to_all x2, blocking collectives, precondition(): lax.all_to_all(field, 'gx', split_axis=2, concat_axis=0, tiled=True)  372 us
    all_to_all x2, blocking collectives, precondition(): lax.all_to_all(hat, 'gx', split_axis=0, concat_axis=2, tiled=True)  372 us
    all_to_all x1, blocking collectives, precondition(): lax.all_to_all(lax.all_to_all(field, 'gx', split_axis=2, concat_axis=0, t...  97.9 us
    all_to_all x1, blocking collectives, precondition(): lax.all_to_all(lax.all_to_all(hat, 'gx', split_axis=0, concat_axis=2, til...  97.8 us
    mul x6, other arithmetic, smooth_axis(): 0.25 * (cut(field, 0, length - 2, axis) + 2.0 * cut(field, 1, length - 1,...  96.6 us
    all_to_all x1, waiting for transfers between devices, precondition(): lax.all_to_all(lax.all_to_all(hat, 'gx', split_axis=0, concat_axis=2, til...  94.1 us
    all_to_all x1, waiting for transfers between devices, precondition(): lax.all_to_all(lax.all_to_all(field, 'gx', split_axis=2, concat_axis=0, t...  94 us
    psum x2, blocking collectives, inner(): return lax.psum(jnp.sum(first * second), ('gx', 'gy'))  79.7 us
  transfers between devices with their start and end apart: 14, of which 9 were waited for; matrix products, arithmetic and copies ran while one was open for 0% of the time, Pallas kernels for 0%

commit v1 on v0

--- a/solution.py
+++ b/solution.py
@@ -1,5 +1,6 @@
 import jax
 import jax.numpy as jnp
+import numpy as np
 from jax import lax
 from jax.sharding import PartitionSpec as P
 
@@ -61,15 +62,136 @@
 
 
 def cosine_table(order):
-    freq = jnp.arange(order, dtype=jnp.float32)[:, None]
-    place = jnp.arange(order, dtype=jnp.float32)[None, :]
-    scale = jnp.where(freq == 0.0, jnp.sqrt(1.0 / order), jnp.sqrt(2.0 / order)).astype(jnp.float32)
-    return scale * jnp.cos(jnp.pi * (place + 0.5) * freq / order)
+    freq = np.arange(order, dtype=np.float64)[:, None]
+    place = np.arange(order, dtype=np.float64)[None, :]
+    scale = np.where(freq == 0.0, np.sqrt(1.0 / order), np.sqrt(2.0 / order))
+    return scale * np.cos(np.pi * (place + 0.5) * freq / order)
 
 
 def eigen_values(order):
-    freq = jnp.arange(order, dtype=jnp.float32)
-    return 2.0 - 2.0 * jnp.cos(jnp.pi * freq / order)
+    return 2.0 - 2.0 * np.cos(np.pi * np.arange(order, dtype=np.float64) / order)
+
+
+def axis_tables(order, parts):
+    rows = order // parts
+    whole = cosine_table(order)
+    local = cosine_table(rows)
+    lift = np.concatenate(
+        [local @ whole[:, part * rows : (part + 1) * rows].T for part in range(parts)], axis=0
+    )
+    ends = np.arange(1, parts) * rows - 1
+    jump = (whole[:, ends] - whole[:, ends + 1]).T
+    return local, eigen_values(rows), lift, jump
+
+
+def solver_tables(order_x, order_y, parts_x, parts_y):
+    local_x, near_x, lift_x, jump_x = axis_tables(order_x, parts_x)
+    local_y, near_y, lift_y, jump_y = axis_tables(order_y, parts_y)
+    inverse = 1.0 / (damping + eigen_values(order_x)[:, None] + eigen_values(order_y)[None, :])
+    tables = {
+        "local_x": local_x,
+        "local_y": local_y,
+        "near": 1.0 / (damping + near_x[:, None] + near_y[None, :]),
+        "lift_x": lift_x,
+        "lift_y": lift_y,
+        "jump_x": jump_x,
+        "jump_y": jump_y,
+        "inverse": inverse,
+        "self_x": np.einsum("ak,bk,kl->abl", jump_x, jump_x, inverse, optimize=True),
+        "self_y": np.einsum("al,bl,kl->abk", jump_y, jump_y, inverse, optimize=True),
+    }
+    return {name: jnp.asarray(value.astype(np.float32)) for name, value in tables.items()}
+
+
+def product(first, second):
+    return lax.dot_general(
+        first,
+        second,
+        (((first.ndim - 1,), (0,)), ((), ())),
+        precision=highest,
+        preferred_element_type=jnp.float32,
+    )
+
+
+def solve_borders(jumps_x, jumps_y, tables):
+    hat_x = product(jumps_x, tables["lift_y"])
+    hat_y = product(jumps_y, tables["lift_x"])
+    jump_x, jump_y = tables["jump_x"], tables["jump_y"]
+    cross_x = product(jump_x[:, None, None, :] * hat_y[None], tables["inverse"])
+    cross_y = product(jump_y[None, :, None, :] * hat_x[:, None], tables["inverse"].T)
+    flux_x = (
+        hat_x
+        - jnp.sum(tables["self_x"][:, :, None, :] * hat_x[None], axis=1)
+        - jnp.sum(jump_y[None, :, None, :] * cross_x, axis=1)
+    )
+    flux_y = (
+        hat_y
+        - jnp.sum(tables["self_y"][:, :, None, :] * hat_y[None], axis=1)
+        - jnp.sum(jump_x[:, None, None, :] * cross_y, axis=0)
+    )
+    return product(flux_x, tables["lift_y"].T), product(flux_y, tables["lift_x"].T)
+
+
+def exchange(rows):
+    return lax.all_to_all(rows, ("gx", "gy"), split_axis=0, concat_axis=0, tiled=True)
+
+
+def forward(field, tables):
+    hat = jnp.einsum("ki,ijt->kjt", tables["local_x"], field, precision=highest)
+    return jnp.einsum("lj,kjt->klt", tables["local_y"], hat, precision=highest)
+
+
+def backward(hat, tables):
+    field = jnp.einsum("lj,klt->kjt", tables["local_y"], hat, precision=highest)
+    return jnp.einsum("ki,kjt->ijt", tables["local_x"], field, precision=highest)
+
+
+def precondition(field, tables, parts_x, parts_y):
+    rows_x, rows_y, depth = field.shape
+    per = depth // (parts_x * parts_y)
+    near = tables["near"][:, :, None]
+    first_x, last_x = tables["local_x"][:, 0], tables["local_x"][:, -1]
+    first_y, last_y = tables["local_y"][:, 0], tables["local_y"][:, -1]
+    hat = forward(field, tables)
+    free = hat * near
+    edges = jnp.concatenate(
+        [
+            jnp.sum(free * first_x[:, None, None], axis=0),
+            jnp.sum(free * last_x[:, None, None], axis=0),
+            jnp.sum(free * first_y[None, :, None], axis=1),
+            jnp.sum(free * last_y[None, :, None], axis=1),
+        ],
+        axis=0,
+    )
+    got = exchange(edges.T).reshape(parts_x, parts_y, per, 2 * rows_x + 2 * rows_y)
+    low_x, high_x = got[..., :rows_y], got[..., rows_y : 2 * rows_y]
+    low_y, high_y = got[..., 2 * rows_y : 2 * rows_y + rows_x], got[..., 2 * rows_y + rows_x :]
+    jumps_x = (high_x[:-1] - low_x[1:]).transpose(0, 2, 1, 3)
+    jumps_y = (high_y[:, :-1] - low_y[:, 1:]).transpose(1, 2, 0, 3)
+    flux_x, flux_y = solve_borders(
+        jumps_x.reshape(parts_x - 1, per, -1), jumps_y.reshape(parts_y - 1, per, -1), tables
+    )
+    flux_x = flux_x.reshape(parts_x - 1, per, parts_y, rows_y).transpose(0, 2, 1, 3)
+    flux_y = flux_y.reshape(parts_y - 1, per, parts_x, rows_x).transpose(2, 0, 1, 3)
+    sent = jnp.concatenate(
+        [
+            jnp.pad(-flux_x, ((1, 0), (0, 0), (0, 0), (0, 0))),
+            jnp.pad(flux_x, ((0, 1), (0, 0), (0, 0), (0, 0))),
+            jnp.pad(-flux_y, ((0, 0), (1, 0), (0, 0), (0, 0))),
+            jnp.pad(flux_y, ((0, 0), (0, 1), (0, 0), (0, 0))),
+        ],
+        axis=-1,
+    )
+    back = exchange(sent.reshape(depth, -1)).T
+    solved = near * (
+        hat
+        - first_x[:, None, None] * back[None, :rows_y]
+        - last_x[:, None, None] * back[None, rows_y : 2 * rows_y]
+        - first_y[None, :, None] * back[2 * rows_y : 2 * rows_y + rows_x, None]
+        - last_y[None, :, None] * back[2 * rows_y + rows_x :, None]
+    )
+    norm = lax.psum(jnp.sum(hat * solved), ("gx", "gy"))
+    return backward(solved, tables), norm
 
 
 def combine_terms(field, upper_x, lower_x, upper_y, lower_y, weight_x, weight_y, prior_x, prior_y):
@@ -97,50 +219,18 @@
     )
 
 
-def solve_front(front, table_x, table_y, plane_denom):
-    hat = jnp.einsum("ki,tij->tkj", table_x, front, precision=highest)
-    hat = jnp.einsum("lj,tkj->tkl", table_y, hat, precision=highest)
-    hat = hat / plane_denom
-    hat = jnp.einsum("lj,tkl->tkj", table_y, hat, precision=highest)
-    return jnp.einsum("ki,tkj->tij", table_x, hat, precision=highest)
-
-
-def slice_solve(whole, table_x, table_y, plane_denom):
-    front = jnp.transpose(whole, (2, 0, 1))
-    return jnp.transpose(solve_front(front, table_x, table_y, plane_denom), (1, 2, 0))
-
-
-def reorder_back(back, rows_x, rows_y, parts_x, parts_y, depth):
-    per = depth // (parts_x * parts_y)
-    target = jnp.arange(depth, dtype=jnp.int32)
-    outer = target // (parts_y * per)
-    middle = target // per % parts_y
-    source = middle * (parts_x * per) + outer * per + target % per
-    select = (jnp.arange(depth, dtype=jnp.int32)[:, None] == source[None, :]).astype(jnp.float32)
-    flat = back.reshape(rows_x * rows_y, depth)
-    return jnp.dot(flat, select, precision=highest, preferred_element_type=jnp.float32).reshape(
-        rows_x, rows_y, depth
-    )
-
-
-def inner(first, second):
-    return lax.psum(jnp.sum(first * second), ("gx", "gy"))
-
-
-def solve(rhs, apply_op, precondition):
-    shift_field = jnp.zeros_like(rhs)
+def solve(rhs, apply_op, precond_op):
     residual = rhs
-    precond = precondition(residual)
-    direction = precond
-    norm_now = inner(residual, precond)
+    direction, norm_now = precond_op(residual)
+    shift_field = None
     for step in range(ITERS):
         image = apply_op(direction)
         alpha = norm_now / lax.psum(jnp.sum(direction * image), ("gx", "gy"))
-        shift_field = shift_field + alpha * direction
+        moved = alpha * direction
+        shift_field = moved if shift_field is None else shift_field + moved
         residual = residual - alpha * image
         if step + 1 < ITERS:
-            precond = precondition(residual)
-            norm_next = inner(residual, precond)
+            precond, norm_next = precond_op(residual)
             direction = precond + norm_next / norm_now * direction
             norm_now = norm_next
     return (shift_field, residual)
@@ -152,11 +242,7 @@
     parts_y = lax.axis_size("gy")
     base_x = lax.axis_index("gx") * rows_x
     base_y = lax.axis_index("gy") * rows_y
-    table_x = cosine_table(NX)
-    table_y = cosine_table(NY)
-    eigen_x = eigen_values(NX)
-    eigen_y = eigen_values(NY)
-    plane_denom = damping + eigen_x[:, None] + eigen_y[None, :]
+    tables = solver_tables(rows_x * parts_x, rows_y * parts_y, parts_x, parts_y)
     padded = extended(seismic, (("gx", 0), ("gy", 1)), 3)
     grid_x = base_x + jnp.arange(-2, rows_x + 2, dtype=jnp.int32)
     grid_y = base_y + jnp.arange(-2, rows_y + 2, dtype=jnp.int32)
@@ -177,28 +263,13 @@
     own_y = weight_y[1:-1, 1:-1]
     prior_y = weight_y[1:-1, :-2]
 
-    def precondition(field):
-        whole = lax.all_to_all(
-            lax.all_to_all(field, "gx", split_axis=2, concat_axis=0, tiled=True),
-            "gy",
-            split_axis=2,
-            concat_axis=1,
-            tiled=True,
-        )
-        hat = slice_solve(whole, table_x, table_y, plane_denom)
-        back = lax.all_to_all(
-            lax.all_to_all(hat, "gx", split_axis=0, concat_axis=2, tiled=True),
-            "gy",
-            split_axis=1,
-            concat_axis=2,
-            tiled=True,
-        )
-        return reorder_back(back, rows_x, rows_y, parts_x, parts_y, depth)
+    def precond_op(field):
+        return precondition(field, tables, parts_x, parts_y)
 
     def apply_tiles(field):
         return operate(field, own_x, own_y, prior_x, prior_y)
 
-    return solve(rhs, apply_tiles, precondition)
+    return solve(rhs, apply_tiles, precond_op)
 
 
 def solution(mesh):

time: 2080 us -> 762 us (0.37)
  blocking collectives: 1060 us -> 198 us
  waiting for transfers between devices: 203 us -> 16.1 us
  local copies, waits for them, and re-layouts: 180 us -> 52.8 us
  matrix products: 223 us -> 129 us
  other arithmetic: 354 us -> 324 us
    all_to_all x6 -> x4, blocking collectives: 940 us -> 73.4 us  [exchange(): lax.all_to_all(rows, ('gx', 'gy'), split_axis=0, concat_axis=0, tiled=True)]
    all_to_all x2 -> x0, waiting for transfers between devices: 188 us -> none  [the longest x1 94.1 us: precondition(): lax.all_to_all(lax.all_to_all(hat, 'gx', split_axis=0, concat_axis=2, til...]
    dot_general x10 -> x20, matrix products: 223 us -> 129 us  [the longest x2 38.1 us: forward(): return jnp.einsum('lj,kjt->klt', tables['local_y'], hat, precision=highest)]
    all_to_all x10 -> x0, local copies, waits for them, and re-layouts: 70.1 us -> none  [the longest x4 30.7 us: precondition(): lax.all_to_all(hat, 'gx', split_axis=0, concat_axis=2, tiled=True)]
    unnamed x39 -> x109, local copies, waits for them, and re-layouts: 45.5 us -> 38.7 us
  transfers between devices with their start and end apart: 14 -> 12, of which waited for: 9 -> 8; matrix products, arithmetic and copies ran while one was open for 0% -> 1% of each run, Pallas kernels for 0% -> 0%
where the time goes in v1:
time: 762 us; the launch traced here: 756 us
  other arithmetic  324 us (43%)
  blocking collectives  198 us (26%)
  matrix products  129 us (17%)
  local copies, waits for them, and re-layouts  52.8 us (7%)
  starting transfers between devices  29.5 us (4%)
  waiting for transfers between devices  16.1 us (2%)
    mul x6, other arithmetic, smooth_axis(): 0.25 * (cut(field, 0, length - 2, axis) + 2.0 * cut(field, 1, length - 1,...  96.5 us
    psum x2, blocking collectives, precondition(): norm = lax.psum(jnp.sum(hat * solved), ('gx', 'gy'))  79.4 us
    all_to_all x4, blocking collectives, exchange(): lax.all_to_all(rows, ('gx', 'gy'), split_axis=0, concat_axis=0, tiled=True)  73.4 us
    mul x1, other arithmetic, tensor_fields(): cross_y = smooth_all(grad_y * grad_t)  53.1 us
    reduce_sum x2, other arithmetic, solve(): alpha = norm_now / lax.psum(jnp.sum(direction * image), ('gx', 'gy'))  45.8 us
    mul x1, other arithmetic, per_device(): flux_x = weight_x * dip_x  45.1 us
    psum x1, blocking collectives, solve(): alpha = norm_now / lax.psum(jnp.sum(direction * image), ('gx', 'gy'))  44.9 us
    unnamed x109, local copies, waits for them, and re-layouts  38.7 us
  transfers between devices with their start and end apart: 12, of which 8 were waited for; matrix products, arithmetic and copies ran while one was open for 1% of the time, Pallas kernels for 0%

profile of v1, /device:TPU:0, one launch (start us, length us, event | category | flops | bytes accessed | tf_op | source)
XLA Modules:
  0.0 755.7 jit_solution(138150950227670805)
XLA Ops:
  0.6 8.2 %copy.101 = f32[128,64,256]{2,0,1:T(8,128)S(1)} copy(f32[128,64,256]{2,1,0:T(8,128)} %param.11) | data formatting | bytes 16777216 | tf_op args[0]
  8.9 3.4 copy-done.6
  12.4 4.9 collective-permute-start
  17.3 1.3 collective-permute-start.1
  18.8 4.1 collective-permute-done
  22.8 4.1 collective-permute-done.1
  28.2 1.3 collective-permute-start.2
  29.5 1.5 collective-permute-start.3
  31.7 3.2 collective-permute-done.3
  34.8 3.8 pad_maximum_fusion
  38.7 3.7 copy-done.2
  42.4 4.5 slice.390
  46.9 53.1 %fusion.110 = (f32[132,68,256]{2,0,1:T(8,128)}, f32[132,68,256]{2,0,1:T(8,128)}, f32[132,68,256]{2,0,1:T(8,128)}, f32[132,68,256]{2,0,1:T(8,128)}) fusion(f32[132,68]{0,1:T(8,128)S(1)} %multiply_multiply_fusion, f32[134,70,256]{2,0,1:T(8,128)} %copy-done.2, f32[132,68,256]{2,0,1:T(8,128)} %slice.390), kind=kLoop, calls=%fused_computation.177 | loop fusion | flops 36765696 | bytes 82758720 | tf_op jit(solution)/shard_map/mul | solution.py:58
  100.0 29.4 %fusion.6 = (f32[130,68,256]{2,0,1:T(8,128)}, f32[130,68,256]{2,0,1:T(8,128)}) fusion(f32[132,68,256]{2,0,1:T(8,128)} %get-tuple-element.34, f32[132,68,256]{2,0,1:T(8,128)} %get-tuple-element.35), kind=kLoop, calls=%fused_computation.23 | loop fusion | flops 18104320 | bytes 72417280 | tf_op jit(solution)/shard_map/mul | solution.py:36
  129.4 13.6 %broadcast_multiply_fusion.4 = f32[130,66,256]{2,0,1:T(8,128)} fusion(f32[130,68,256]{2,0,1:T(8,128)} %get-tuple-element.60), kind=kLoop, calls=%fused_computation.153 | loop fusion | flops 8785920 | bytes 35143680 | tf_op jit(solution)/shard_map/mul | solution.py:36
  144.3 5.0 broadcast_multiply_fusion.5
  149.3 29.4 %fusion.2 = (f32[130,68,256]{2,0,1:T(8,128)}, f32[130,68,256]{2,0,1:T(8,128)}) fusion(f32[132,68,256]{2,0,1:T(8,128)} %get-tuple-element.32, f32[132,68,256]{2,0,1:T(8,128)} %get-tuple-element.33), kind=kLoop, calls=%fused_computation.15 | loop fusion | flops 18104320 | bytes 72417280 | tf_op jit(solution)/shard_map/mul | solution.py:36
  178.7 13.7 %broadcast_multiply_fusion.3 = f32[130,66,256]{2,0,1:T(8,128)} fusion(f32[130,68,256]{2,0,1:T(8,128)} %get-tuple-element.59), kind=kLoop, calls=%fused_computation.152 | loop fusion | flops 8785920 | bytes 35143680 | tf_op jit(solution)/shard_map/mul | solution.py:36
  193.6 5.4 broadcast_multiply_fusion.2
  199.1 1.4 slice-done.3
  202.4 45.1 %fusion.24 = (f32[130,66,256]{2,0,1:T(8,128)}, f32[130,66,256]{2,0,1:T(8,128)}, f32[130,66,256]{2,0,1:T(8,128)}, f32[130,66,256]{2,0,1:T(8,128)}) fusion(f32[130,66,256]{2,0,1:T(8,128)} %broadcast_multiply_fusion.3, f32[130,68,256]{2,0,1:T(8,128)} %get-tuple-element.59, f32[130]{0:T(256)S(1)} %and_convert_fusion.1, f32[130,68,256]{2,0,1:T(8,128)S(1)} %bitcast.155, ...), kind=kLoop, calls=%fused_computation.47 | loop fusion | flops 61501440 | bytes 140575232 | tf_op jit(solution)/shard_map/mul | solution.py:258
  247.5 26.8 %fusion.30 = (f32[130,66,256]{2,0,1:T(8,128)}, f32[130,66,256]{2,0,1:T(8,128)}) fusion(f32[130,66,256]{2,0,1:T(8,128)} %get-tuple-element.29, f32[130,66,256]{2,0,1:T(8,128)} %broadcast_multiply_fusion.2, f32[130,68,256]{2,0,1:T(8,128)} %get-tuple-element.58, f32[130,66,256]{2,0,1:T(8,128)} %get-tuple-element.28, f32[66]{0:T(128)S(1)} %copy-done.38), kind=kLoop, calls=%fused_computation.53 | loop fusion | flops 24161280 | bytes 70287624 | tf_op jit(solution)/shard_map/mul | solution.py:259
  274.4 13.2 %fusion.59 = f32[128,64,256]{2,0,1:T(8,128)S(1)} fusion(f32[130,66,256]{2,0,1:T(8,128)} %get-tuple-element.30, f32[130,66,256]{2,0,1:T(8,128)} %get-tuple-element.26), kind=kLoop, calls=%fused_computation.107 | loop fusion | flops 6291456 | bytes 41943040 | tf_op jit(solution)/shard_map/add | solution.py:260
  287.7 8.3 %fusion.152 = f32[128,64,256]{2,0,1:T(8,128)S(1)} fusion(f32[128,128,1]{1,0,2:T(8,128)S(1)} %copy-done.13, f32[128,64,256]{2,0,1:T(8,128)S(1)} %fusion.59), kind=kOutput, calls=%fused_computation.270 | convolution fusion | flops 3221225472 | bytes 16842752 | tf_op jit(solution)/shard_map/ki,ijt->kjt/dot_general | solution.py:140
  296.1 19.0 %multiply_reduce_fusion.9 = (f32[64,256]{1,0:T(8,128)S(1)}, f32[64,256]{1,0:T(8,128)S(1)}, f32[128,256]{1,0:T(8,128)S(1)}, f32[128,256]{1,0:T(8,128)S(1)}, f32[128,256,64]{1,2,0:T(8,128)}) fusion(f32[128]{0:T(128)S(1)} %copy-done.22, f32[128,64]{1,0:T(8,128)S(1)} %copy-done.16, f32[128]{0:T(128)S(1)} %copy-done.26, f32[64]{0:T(128)S(1)} %copy-done.30, ...), kind=kOutput, calls=%fused_computation.146 | convolution fusion | flops 1629388800 | bytes 17221120 | tf_op jit(solution)/shard_map/lj,kjt->klt/dot_general | solution.py:141
  316.1 24.8 %all_to_all.42 = f32[32,8,384]{2,1,0:T(8,128)S(1)} all-to-all(f32[32,8,384]{2,1,0:T(8,128)} %bitcast.168), channel_id=1, replica_groups=mesh['gx'=4,'gy'=8] {'gx','gy'}, dimensions={0} | all-to-all | bytes 786432 | tf_op jit(solution)/shard_map/all_to_all | solution.py:136
  341.8 1.7 fusion.131
  344.9 1.5 fusion.113
  346.5 1.6 fusion.135
  349.0 1.9 fusion.111
  353.1 15.6 %all_to_all.43 = f32[32,8,384]{2,1,0:T(8,128)S(1)} all-to-all(f32[32,8,384]{2,1,0:T(8,128)S(1)} %bitcast.166), channel_id=1, replica_groups=mesh['gx'=4,'gy'=8] {'gx','gy'}, dimensions={0} | all-to-all | bytes 786432 | tf_op jit(solution)/shard_map/all_to_all | solution.py:136
  371.3 1.6 copy.110
  372.9 1.6 copy.111
  374.5 13.1 %fusion.105 = f32[128,64,256]{2,1,0:T(8,128)S(1)} fusion(f32[64,64,1]{1,0,2:T(8,128)} %constant.110, f32[128,256,64]{1,2,0:T(8,128)} %get-tuple-element.56, f32[128,256]{1,0:T(8,128)S(1)} %copy.113, f32[128,256]{1,0:T(8,128)S(1)} %copy.112, f32[64,256]{1,0:T(8,128)} %copy.111, f32[64,256]{1,0:T(8,128)} %copy.110, f32[64]{0:T(128)} %constant.108, ...), kind=kOutput, calls=%fused_computation.174 | convolution fusion | flops 1629487104 | bytes 17221120 | tf_op jit(solution)/shard_map/lj,klt->kjt/dot_general | solution.py:145
  387.6 11.7 %fusion.74 = f32[128,64,256]{2,0,1:T(8,128)S(1)} fusion(f32[128,128,1]{1,0,2:T(8,128)S(1)} %copy-done.14, f32[128,64,256]{2,1,0:T(8,128)S(1)} %fusion.105), kind=kOutput, calls=%fused_computation.129 | convolution fusion | flops 3221225472 | bytes 16842752 | tf_op jit(solution)/shard_map/ki,kjt->ijt/dot_general | solution.py:146
  399.5 1.4 collective-permute-start.4
  400.9 4.5 collective-permute-start.5
  405.8 1.6 collective-permute-done.5
  407.4 1.3 collective-permute-start.6
  408.7 3.0 collective-permute-start.7
  411.8 5.4 fusion.69
  417.2 20.2 %multiply_reduce_fusion.5 = (f32[]{:T(128)}, f32[128,64,256]{2,0,1:T(8,128)}) fusion(f32[128,64,256]{2,0,1:T(8,128)S(1)} %fusion.74, f32[1,64,256]{2,0,1:T(1,128)S(1)} %collective-permute-done.4, f32[1,64,256]{2,0,1:T(1,128)S(1)} %collective-permute-done.5, f32[130,1,256]{2,0,1:T(8,128)S(1)} %collective-permute-done.7, ...), kind=kLoop, calls=%fused_computation.142 | loop fusion | flops 48234496 | bytes 50728964 | tf_op jit(solution)/shard_map/reduce_sum | solution.py:228
  437.4 40.3 %all-reduce.13 = (f32[]{:T(128)}, f32[]{:T(128)}) all-reduce(f32[]{:T(128)} %fusion.69, f32[]{:T(128)} %get-tuple-element.24), channel_id=1, replica_groups=mesh['gx'=4,'gy'=8] {'gx','gy'}, use_global_device_ids=true, to_apply=%region_9.10 | all-reduce | flops 2 | bytes 16 | tf_op jit(solution)/shard_map/psum | solution.py:193
  479.1 11.1 %fusion.108 = f32[128,64,256]{2,0,1:T(8,128)S(1)} fusion(f32[128,128,1]{1,0,2:T(8,128)S(1)} %copy-done.14, f32[128,64,256]{2,0,1:T(8,128)} %copy-done.5, f32[128,64,256]{2,0,1:T(8,128)} %get-tuple-element.25, f32[]{:T(128)S(6)} %div.21), kind=kOutput, calls=%fused_computation.175 | convolution fusion | flops 3225419776 | bytes 25231364 | tf_op jit(solution)/shard_map/ki,ijt->kjt/dot_general | solution.py:140
  490.3 19.0 %multiply_reduce_fusion.4 = (f32[64,256]{1,0:T(8,128)S(1)}, f32[64,256]{1,0:T(8,128)S(1)}, f32[128,256]{1,0:T(8,128)S(1)}, f32[128,256]{1,0:T(8,128)S(1)}, f32[128,256,64]{1,2,0:T(8,128)}) fusion(f32[128]{0:T(128)S(1)} %copy-done.24, f32[128,64]{1,0:T(8,128)S(1)} %copy-done.17, f32[128]{0:T(128)S(1)} %copy-done.28, f32[64]{0:T(128)S(1)} %copy-done.32, ...), kind=kOutput, calls=%fused_computation.140 | convolution fusion | flops 1629388800 | bytes 17221120 | tf_op jit(solution)/shard_map/lj,kjt->klt/dot_general | solution.py:141
  510.3 17.4 %all_to_all.44 = f32[32,8,384]{2,1,0:T(8,128)S(1)} all-to-all(f32[32,8,384]{2,1,0:T(8,128)} %bitcast.169), channel_id=1, replica_groups=mesh['gx'=4,'gy'=8] {'gx','gy'}, dimensions={0} | all-to-all | bytes 786432 | tf_op jit(solution)/shard_map/all_to_all | solution.py:136
  530.1 1.5 fusion.114
  532.7 1.9 fusion.112
  536.8 15.6 %all_to_all.45 = f32[32,8,384]{2,1,0:T(8,128)S(1)} all-to-all(f32[32,8,384]{2,1,0:T(8,128)S(1)} %bitcast.167), channel_id=1, replica_groups=mesh['gx'=4,'gy'=8] {'gx','gy'}, dimensions={0} | all-to-all | bytes 786432 | tf_op jit(solution)/shard_map/all_to_all | solution.py:136
  553.0 7.3 fusion.64
  560.4 14.3 %fusion.102 = f32[128,64,256]{2,1,0:T(8,128)} fusion(f32[64,64,1]{1,0,2:T(8,128)S(1)} %copy-done.41, f32[128,256,64]{1,2,0:T(8,128)} %get-tuple-element.57, f32[128,256]{1,0:T(8,128)S(1)} %copy.126, f32[128,256]{1,0:T(8,128)S(1)} %copy.125, f32[64,256]{1,0:T(8,128)S(1)} %copy.124, f32[64,256]{1,0:T(8,128)S(1)} %copy.123, f32[64]{0:T(128)S(1)} %copy-done.37, ...), kind=kOutput, calls=%fused_computation.173 | convolution fusion | flops 1629487104 | bytes 17221120 | tf_op jit(solution)/shard_map/lj,klt->kjt/dot_general | solution.py:145
  574.7 39.1 %psum.30 = f32[]{:T(128)} all-reduce(f32[]{:T(128)} %fusion.64), channel_id=1, replica_groups=mesh['gx'=4,'gy'=8] {'gx','gy'}, use_global_device_ids=true, to_apply=%region_21.22 | all-reduce | flops 1 | bytes 8 | tf_op jit(solution)/shard_map/psum | solution.py:193
  615.1 17.4 %multiply_add_fusion.2 = f32[128,64,256]{2,0,1:T(8,128)S(1)} fusion(f32[128,64,256]{2,0,1:T(8,128)} %copy-done.3, f32[]{:T(128)S(6)} %div.22, f32[128,128,1]{1,0,2:T(8,128)S(1)} %copy-done.15, f32[128,64,256]{2,1,0:T(8,128)} %fusion.102), kind=kOutput, calls=%fused_computation.136 | convolution fusion | flops 3225419776 | bytes 25231364 | tf_op jit(solution)/shard_map/ki,kjt->ijt/dot_general | solution.py:146
  632.6 1.3 collective-permute-start.8
  633.9 4.5 collective-permute-start.9
  638.8 1.6 collective-permute-done.9
  640.4 1.3 collective-permute-start.10
  641.7 3.0 collective-permute-start.11
  645.7 25.6 %multiply_reduce_fusion = (f32[]{:T(128)}, f32[128,64,256]{2,0,1:T(8,128)}) fusion(f32[128,64,256]{2,0,1:T(8,128)} %copy-done.4, f32[1,64,256]{2,0,1:T(1,128)S(1)} %collective-permute-done.8, f32[1,64,256]{2,0,1:T(1,128)S(1)} %collective-permute-done.9, f32[130,1,256]{2,0,1:T(8,128)S(1)} %collective-permute-done.11, f32[130,66,256]{2,0,1:T(8,128)S(1)} %bitcast.159, ...), kind=kLoop, calls=%fused_computation.135 | loop fusion | flops 48234496 | bytes 50728964 | tf_op jit(solution)/shard_map/reduce_sum | solution.py:228
  671.4 44.9 %psum.31 = f32[]{:T(128)} all-reduce(f32[]{:T(128)} %get-tuple-element.22), channel_id=1, replica_groups=mesh['gx'=4,'gy'=8] {'gx','gy'}, use_global_device_ids=true, to_apply=%region_23.24 | all-reduce | flops 1 | bytes 8 | tf_op jit(solution)/shard_map/psum | solution.py:228
  717.5 11.8 %multiply_add_fusion.1 = f32[128,64,256]{2,0,1:T(8,128)} fusion(f32[128,64,256]{2,0,1:T(8,128)} %copy-done.4, f32[128,64,256]{2,0,1:T(8,128)} %copy-done.3, f32[]{:T(128)S(6)} %div.23, f32[]{:T(128)S(6)} %div.21), kind=kLoop, calls=%fused_computation.134 | loop fusion | flops 6291456 | bytes 25165832 | tf_op jit(solution)/shard_map/add | solution.py:230
  729.3 9.4 %multiply_subtract_fusion = f32[128,64,256]{2,0,1:T(8,128)S(1)} fusion(f32[128,64,256]{2,0,1:T(8,128)} %get-tuple-element.23, f32[]{:T(128)S(6)} %div.23, f32[128,64,256]{2,0,1:T(8,128)} %copy-done.5, f32[128,64,256]{2,0,1:T(8,128)} %get-tuple-element.25, f32[]{:T(128)S(6)} %div.21), kind=kLoop, calls=%fused_computation.133 | loop fusion | flops 8388608 | bytes 33554440 | tf_op jit(solution)/shard_map/sub | solution.py:231
  738.7 8.3 %copy.131 = f32[128,64,256]{2,1,0:T(8,128)} copy(f32[128,64,256]{2,0,1:T(8,128)S(1)} %multiply_subtract_fusion) | data formatting | bytes 16777216
  747.0 8.3 %copy.130 = f32[128,64,256]{2,1,0:T(8,128)} copy(f32[128,64,256]{2,0,1:T(8,128)S(1)} %copy-done.8) | data formatting | bytes 16777216
  (169 shorter events, 24.5 us)
Async XLA Ops:
  8.9 3.4 copy-start.6
  12.4 10.5 %collective-permute-start = (f32[3,64,256]{2,0,1:T(4,128)S(1)}, f32[3,64,256]{2,0,1:T(4,128)S(1)}, u32[]{:S(2)}, u32[]{:S(2)}) collective-permute-start(f32[3,64,256]{2,0,1:T(4,128)S(1)} %get-tuple-element.46), channel_id=1, source_target_pairs={{0,8},{8,16},{16,24},{1,9},{9,17},{17,25},{2,10},{10,18},{18,26},{... | collective-permute-start | bytes 589832 | tf_op jit(solution)/shard_map/ppermute | solution.py:22
  17.3 9.7 %collective-permute-start.1 = (f32[3,64,256]{2,0,1:T(4,128)S(1)}, f32[3,64,256]{2,0,1:T(4,128)S(1)}, u32[]{:S(2)}, u32[]{:S(2)}) collective-permute-start(f32[3,64,256]{2,0,1:T(4,128)S(1)} %get-tuple-element.47), channel_id=1, source_target_pairs={{8,0},{16,8},{24,16},{9,1},{17,9},{25,17},{10,2},{18,10},{26,18},{... | collective-permute-start | bytes 589832 | tf_op jit(solution)/shard_map/ppermute | solution.py:25
  18.7 16.2 %copy-start.7 = (f32[128,64,256]{2,0,1:T(8,128)S(1)}, f32[128,64,256]{2,0,1:T(8,128)}, u32[]{:S(2)}) copy-start(f32[128,64,256]{2,0,1:T(8,128)} %copy-done.6) | copy-start | bytes 25165828
  28.2 3.5 collective-permute-start.2
  29.5 5.4 collective-permute-start.3
  38.7 3.7 copy-start.2
  129.4 14.9 %copy-start = (f32[130,68,256]{2,0,1:T(8,128)S(1)}, f32[130,68,256]{2,0,1:T(8,128)}, u32[]{:S(2)}) copy-start(f32[130,68,256]{2,0,1:T(8,128)} %get-tuple-element.61) | copy-start | bytes 27156484
  178.7 14.9 %copy-start.1 = (f32[130,68,256]{2,0,1:T(8,128)S(1)}, f32[130,68,256]{2,0,1:T(8,128)}, u32[]{:S(2)}) copy-start(f32[130,68,256]{2,0,1:T(8,128)} %get-tuple-element.58) | copy-start | bytes 27156484
  178.7 20.3 %slice-start = ((s8[9469952]{0:T(1024)(128)(4,1)}), s8[4194304]{0:T(1024)(128)(4,1)S(1)}, s32[]{:S(2)}) async-start(s8[9469952]{0:T(1024)(128)(4,1)} %bitcast.154), calls=%async_computation.4 | async-start | bytes 8388608
  178.7 20.3 %slice-start.1 = ((s8[9469952]{0:T(1024)(128)(4,1)}), s8[4194304]{0:T(1024)(128)(4,1)S(1)}, s32[]{:S(2)}) async-start(s8[9469952]{0:T(1024)(128)(4,1)} %bitcast.154), calls=%async_computation.5 | async-start | bytes 8388608
  178.7 21.7 %slice-start.3 = ((s8[9469952]{0:T(1024)(128)(4,1)}), s8[4194304]{0:T(1024)(128)(4,1)S(1)}, s32[]{:S(2)}) async-start(s8[9469952]{0:T(1024)(128)(4,1)} %bitcast.156), calls=%async_computation.7 | async-start | bytes 8388608
  178.7 22.9 %slice-start.4 = ((s8[9469952]{0:T(1024)(128)(4,1)}), s8[4194304]{0:T(1024)(128)(4,1)S(1)}, s32[]{:S(2)}) async-start(s8[9469952]{0:T(1024)(128)(4,1)} %bitcast.156), calls=%async_computation.8 | async-start | bytes 8388608
  193.6 8.5 %slice-start.2 = ((s8[9469952]{0:T(1024)(128)(4,1)}), s8[1081344]{0:T(1024)(128)(4,1)S(1)}, s32[]{:S(2)}) async-start(s8[9469952]{0:T(1024)(128)(4,1)} %bitcast.154), calls=%async_computation.6 | async-start | bytes 2162688
  193.6 8.8 %slice-start.5 = ((s8[9469952]{0:T(1024)(128)(4,1)}), s8[1081344]{0:T(1024)(128)(4,1)S(1)}, s32[]{:S(2)}) async-start(s8[9469952]{0:T(1024)(128)(4,1)} %bitcast.156), calls=%async_computation.9 | async-start | bytes 2162688
  202.4 45.1 %copy-start.38 = (f32[66]{0:T(128)S(1)}, f32[66]{0:T(128)}, u32[]{:S(2)}) copy-start(f32[66]{0:T(128)} %and_convert_fusion) | copy-start | bytes 796
  274.4 13.2 %copy-start.13 = (f32[128,128,1]{1,0,2:T(8,128)S(1)}, f32[128,128,1]{1,0,2:T(8,128)}, u32[]{:S(2)}) copy-start(f32[128,128,1]{1,0,2:T(8,128)} %constant.109) | copy-start | bytes 196612
  287.6 8.4 %copy-start.5 = (f32[128,64,256]{2,0,1:T(8,128)}, f32[128,64,256]{2,0,1:T(8,128)S(1)}, u32[]{:S(2)}) copy-start(f32[128,64,256]{2,0,1:T(8,128)S(1)} %fusion.59) | copy-start | bytes 25165828
  287.6 8.4 %copy-start.16 = (f32[128,64]{1,0:T(8,128)S(1)}, f32[128,64]{1,0:T(8,128)}, u32[]{:S(2)}) copy-start(f32[128,64]{1,0:T(8,128)} %constant.22.clone) | copy-start | bytes 98308
  287.6 8.4 %copy-start.22 = (f32[128]{0:T(128)S(1)}, f32[128]{0:T(128)}, u32[]{:S(2)}) copy-start(f32[128]{0:T(128)} %constant.102) | copy-start | bytes 1540
  287.6 8.4 %copy-start.26 = (f32[128]{0:T(128)S(1)}, f32[128]{0:T(128)}, u32[]{:S(2)}) copy-start(f32[128]{0:T(128)} %constant.104) | copy-start | bytes 1540
  287.6 8.4 %copy-start.30 = (f32[64]{0:T(128)S(1)}, f32[64]{0:T(128)}, u32[]{:S(2)}) copy-start(f32[64]{0:T(128)} %constant.106) | copy-start | bytes 772
  287.6 8.4 %copy-start.34 = (f32[64]{0:T(128)S(1)}, f32[64]{0:T(128)}, u32[]{:S(2)}) copy-start(f32[64]{0:T(128)} %constant.108) | copy-start | bytes 772
  287.6 8.4 %copy-start.39 = (f32[64,64,1]{1,0,2:T(8,128)S(1)}, f32[64,64,1]{1,0,2:T(8,128)}, u32[]{:S(2)}) copy-start(f32[64,64,1]{1,0,2:T(8,128)} %constant.110) | copy-start | bytes 49156
  296.0 45.8 %copy-start.10 = (f32[512,512,1]{1,0,2:T(8,128)S(1)}, f32[512,512,1]{1,0,2:T(8,128)}, u32[]{:S(2)}) copy-start(f32[512,512,1]{1,0,2:T(8,128)} %constant.112) | copy-start | bytes 3145732
  296.1 47.5 %copy-start.11 = (f32[512,512,1]{1,0,2:T(8,128)S(1)}, f32[512,512,1]{1,0,2:T(8,128)}, u32[]{:S(2)}) copy-start(f32[512,512,1]{1,0,2:T(8,128)} %constant.111) | copy-start | bytes 3145732
  296.1 48.8 %copy-start.9 = (f32[512,512,1,1]{1,0,3,2:T(8,128)S(1)}, f32[512,512,1,1]{1,0,3,2:T(8,128)}, u32[]{:S(2)}) copy-start(f32[512,512,1,1]{1,0,3,2:T(8,128)} %constant.113) | copy-start | bytes 3145732
  296.1 48.8 %copy-start.19 = (f32[7,512]{1,0:T(8,128)S(1)}, f32[7,512]{1,0:T(8,128)}, u32[]{:S(2)}) copy-start(f32[7,512]{1,0:T(8,128)} %constant.71.clone) | copy-start | bytes 43012
  316.1 58.4 %copy-start.17 = (f32[128,64]{1,0:T(8,128)S(1)}, f32[128,64]{1,0:T(8,128)}, u32[]{:S(2)}) copy-start(f32[128,64]{1,0:T(8,128)} %constant.22.clone) | copy-start | bytes 98308
  374.5 13.1 %copy-start.14 = (f32[128,128,1]{1,0,2:T(8,128)S(1)}, f32[128,128,1]{1,0,2:T(8,128)}, u32[]{:S(2)}) copy-start(f32[128,128,1]{1,0,2:T(8,128)} %constant.109) | copy-start | bytes 196612
  374.5 37.2 %slice-start.9 = ((s8[8388608]{0:T(1024)(128)(4,1)}), s8[4194304]{0:T(1024)(128)(4,1)S(1)}, s32[]{:S(2)}) async-start(s8[8388608]{0:T(1024)(128)(4,1)} %bitcast.160), calls=%async_computation.13 | async-start | bytes 8388608
  387.6 24.1 %slice-start.10 = ((s8[8388608]{0:T(1024)(128)(4,1)}), s8[4194304]{0:T(1024)(128)(4,1)S(1)}, s32[]{:S(2)}) async-start(s8[8388608]{0:T(1024)(128)(4,1)} %bitcast.160), calls=%async_computation.14 | async-start | bytes 8388608
  399.3 17.9 %copy-start.3 = (f32[128,64,256]{2,0,1:T(8,128)}, f32[128,64,256]{2,0,1:T(8,128)S(1)}, u32[]{:S(2)}) copy-start(f32[128,64,256]{2,0,1:T(8,128)S(1)} %fusion.74) | copy-start | bytes 25165828
  399.3 12.4 %copy-start.20 = (f32[64,256]{1,0:T(8,128)S(1)}, f32[64,256]{1,0:T(8,128)}, u32[]{:S(2)}) copy-start(f32[64,256]{1,0:T(8,128)} %copy.110) | copy-start | bytes 196612
  399.3 12.4 %copy-start.21 = (f32[64,256]{1,0:T(8,128)S(1)}, f32[64,256]{1,0:T(8,128)}, u32[]{:S(2)}) copy-start(f32[64,256]{1,0:T(8,128)} %copy.111) | copy-start | bytes 196612
  399.3 12.4 %copy-start.23 = (f32[128]{0:T(128)S(1)}, f32[128]{0:T(128)}, u32[]{:S(2)}) copy-start(f32[128]{0:T(128)} %constant.102) | copy-start | bytes 1540
  399.4 12.4 %copy-start.27 = (f32[128]{0:T(128)S(1)}, f32[128]{0:T(128)}, u32[]{:S(2)}) copy-start(f32[128]{0:T(128)} %constant.104) | copy-start | bytes 1540
  399.4 12.4 %copy-start.31 = (f32[64]{0:T(128)S(1)}, f32[64]{0:T(128)}, u32[]{:S(2)}) copy-start(f32[64]{0:T(128)} %constant.106) | copy-start | bytes 772
  399.4 12.4 %copy-start.35 = (f32[64]{0:T(128)S(1)}, f32[64]{0:T(128)}, u32[]{:S(2)}) copy-start(f32[64]{0:T(128)} %constant.108) | copy-start | bytes 772
  399.5 6.3 collective-permute-start.4
  400.9 6.4 collective-permute-start.5
  407.4 9.8 %collective-permute-start.6 = (f32[130,1,256]{2,0,1:T(8,128)S(1)}, f32[130,1,256]{2,0,1:T(8,128)S(1)}, u32[]{:S(2)}, u32[]{:S(2)}) collective-permute-start(f32[130,1,256]{2,0,1:T(8,128)S(1)} %get-tuple-element.40), channel_id=1, source_target_pairs={{1,0},{2,1},{3,2},{4,3},{5,4},{6,5},{7,6},{9,8},{10,9},{11,10},{12... | collective-permute-start | bytes 399368 | tf_op jit(solution)/shard_map/ppermute | solution.py:25
  408.7 8.5 %collective-permute-start.7 = (f32[130,1,256]{2,0,1:T(8,128)S(1)}, f32[130,1,256]{2,0,1:T(8,128)S(1)}, u32[]{:S(2)}, u32[]{:S(2)}) collective-permute-start(f32[130,1,256]{2,0,1:T(8,128)S(1)} %get-tuple-element.41), channel_id=1, source_target_pairs={{0,1},{1,2},{2,3},{3,4},{4,5},{5,6},{6,7},{8,9},{9,10},{10,11},{11... | collective-permute-start | bytes 399368 | tf_op jit(solution)/shard_map/ppermute | solution.py:22
  479.0 11.2 %copy-start.24 = (f32[128]{0:T(128)S(1)}, f32[128]{0:T(128)}, u32[]{:S(2)}) copy-start(f32[128]{0:T(128)} %constant.102) | copy-start | bytes 1540
  479.0 11.2 %copy-start.28 = (f32[128]{0:T(128)S(1)}, f32[128]{0:T(128)}, u32[]{:S(2)}) copy-start(f32[128]{0:T(128)} %constant.104) | copy-start | bytes 1540
  479.0 11.2 %copy-start.32 = (f32[64]{0:T(128)S(1)}, f32[64]{0:T(128)}, u32[]{:S(2)}) copy-start(f32[64]{0:T(128)} %constant.106) | copy-start | bytes 772
  479.0 11.2 %copy-start.36 = (f32[64]{0:T(128)S(1)}, f32[64]{0:T(128)}, u32[]{:S(2)}) copy-start(f32[64]{0:T(128)} %constant.108) | copy-start | bytes 772
  479.1 11.2 %copy-start.40 = (f32[64,64,1]{1,0,2:T(8,128)S(1)}, f32[64,64,1]{1,0,2:T(8,128)}, u32[]{:S(2)}) copy-start(f32[64,64,1]{1,0,2:T(8,128)} %constant.110) | copy-start | bytes 49156
  510.3 42.7 %copy-start.18 = (f32[128,64]{1,0:T(8,128)S(1)}, f32[128,64]{1,0:T(8,128)}, u32[]{:S(2)}) copy-start(f32[128,64]{1,0:T(8,128)} %constant.22.clone) | copy-start | bytes 98308
  510.3 42.7 %copy-start.25 = (f32[128]{0:T(128)S(1)}, f32[128]{0:T(128)}, u32[]{:S(2)}) copy-start(f32[128]{0:T(128)} %constant.102) | copy-start | bytes 1540
  510.3 42.7 %copy-start.29 = (f32[128]{0:T(128)S(1)}, f32[128]{0:T(128)}, u32[]{:S(2)}) copy-start(f32[128]{0:T(128)} %constant.104) | copy-start | bytes 1540
  510.3 42.7 %copy-start.33 = (f32[64]{0:T(128)S(1)}, f32[64]{0:T(128)}, u32[]{:S(2)}) copy-start(f32[64]{0:T(128)} %constant.106) | copy-start | bytes 772
  510.3 42.7 %copy-start.37 = (f32[64]{0:T(128)S(1)}, f32[64]{0:T(128)}, u32[]{:S(2)}) copy-start(f32[64]{0:T(128)} %constant.108) | copy-start | bytes 772
  532.6 27.8 %copy-start.41 = (f32[64,64,1]{1,0,2:T(8,128)S(1)}, f32[64,64,1]{1,0,2:T(8,128)}, u32[]{:S(2)}) copy-start(f32[64,64,1]{1,0,2:T(8,128)} %constant.110) | copy-start | bytes 49156
  560.3 54.7 %copy-start.15 = (f32[128,128,1]{1,0,2:T(8,128)S(1)}, f32[128,128,1]{1,0,2:T(8,128)}, u32[]{:S(2)}) copy-start(f32[128,128,1]{1,0,2:T(8,128)} %constant.109) | copy-start | bytes 196612
  613.7 32.0 %slice-start.6 = ((s8[9191424]{0:T(1024)(128)(4,1)}), s8[802816]{0:T(1024)(128)(4,1)S(1)}, s32[]{:S(2)}) async-start(s8[9191424]{0:T(1024)(128)(4,1)} %bitcast.158), calls=%async_computation.10 | async-start | bytes 1605632
  615.1 30.7 %slice-start.7 = ((s8[9191424]{0:T(1024)(128)(4,1)}), s8[4194304]{0:T(1024)(128)(4,1)S(1)}, s32[]{:S(2)}) async-start(s8[9191424]{0:T(1024)(128)(4,1)} %bitcast.158), calls=%async_computation.11 | async-start | bytes 8388608
  615.1 30.7 %slice-start.8 = ((s8[9191424]{0:T(1024)(128)(4,1)}), s8[4194304]{0:T(1024)(128)(4,1)S(1)}, s32[]{:S(2)}) async-start(s8[9191424]{0:T(1024)(128)(4,1)} %bitcast.158), calls=%async_computation.12 | async-start | bytes 8388608
  632.5 7.9 %copy-start.4 = (f32[128,64,256]{2,0,1:T(8,128)}, f32[128,64,256]{2,0,1:T(8,128)S(1)}, u32[]{:S(2)}) copy-start(f32[128,64,256]{2,0,1:T(8,128)S(1)} %multiply_add_fusion.2) | copy-start | bytes 25165828
  632.6 6.2 collective-permute-start.8
  633.9 6.4 collective-permute-start.9
  640.4 4.3 collective-permute-start.10
  641.7 4.0 collective-permute-start.11
  738.7 8.3 %copy-start.8 = (f32[128,64,256]{2,0,1:T(8,128)S(1)}, f32[128,64,256]{2,0,1:T(8,128)}, u32[]{:S(2)}) copy-start(f32[128,64,256]{2,0,1:T(8,128)} %multiply_add_fusion.1) | copy-start | bytes 25165828
  (1 other events, 0.7 us)

commit v2 on v1

--- a/solution.py
+++ b/solution.py
@@ -190,8 +190,7 @@
         - first_y[None, :, None] * back[2 * rows_y : 2 * rows_y + rows_x, None]
         - last_y[None, :, None] * back[2 * rows_y + rows_x :, None]
     )
-    norm = lax.psum(jnp.sum(hat * solved), ("gx", "gy"))
-    return backward(solved, tables), norm
+    return backward(solved, tables), jnp.sum(hat * solved)
 
 
 def combine_terms(field, upper_x, lower_x, upper_y, lower_y, weight_x, weight_y, prior_x, prior_y):
@@ -219,18 +218,31 @@
     )
 
 
+def totals(*partials):
+    count = lax.axis_size("gx") * lax.axis_size("gy")
+    rows = jnp.broadcast_to(jnp.stack(partials)[None, :, None], (count, len(partials), 128))
+    return jnp.sum(exchange(rows), axis=0)[:, 0]
+
+
 def solve(rhs, apply_op, precond_op):
     residual = rhs
-    direction, norm_now = precond_op(residual)
+    direction, part = precond_op(residual)
+    norm_now = None
     shift_field = None
     for step in range(ITERS):
         image = apply_op(direction)
-        alpha = norm_now / lax.psum(jnp.sum(direction * image), ("gx", "gy"))
+        curve = jnp.sum(direction * image)
+        if norm_now is None:
+            norm_now, curve = totals(part, curve)
+        else:
+            (curve,) = totals(curve)
+        alpha = norm_now / curve
         moved = alpha * direction
         shift_field = moved if shift_field is None else shift_field + moved
         residual = residual - alpha * image
         if step + 1 < ITERS:
-            precond, norm_next = precond_op(residual)
+            precond, part = precond_op(residual)
+            (norm_next,) = totals(part)
             direction = precond + norm_next / norm_now * direction
             norm_now = norm_next
     return (shift_field, residual)

time: 762 us -> 669 us (0.88)
  blocking collectives: 198 us -> 99.6 us
    psum x3 -> x0, blocking collectives: 124 us -> none  [the longest x2 79.4 us: precondition(): norm = lax.psum(jnp.sum(hat * solved), ('gx', 'gy'))]
    all_to_all x4 -> x6, blocking collectives: 73.4 us -> 99.6 us  [exchange(): lax.all_to_all(rows, ('gx', 'gy'), split_axis=0, concat_axis=0, tiled=True)]
    reduce_sum x4 -> x7, other arithmetic: 58.5 us -> 58.6 us  [the longest x2 45.8 us: solve(): curve = jnp.sum(direction * image)]
  transfers between devices with their start and end apart: 12 -> 13, of which waited for: 8 -> 8; matrix products, arithmetic and copies ran while one was open for 1% -> 3% of each run, Pallas kernels for 0% -> 0%
where the time goes in v2:
time: 669 us; the launch traced here: 663 us
  other arithmetic  326 us (49%)
  matrix products  129 us (19%)
  blocking collectives  99.6 us (15%)
  local copies, waits for them, and re-layouts  55.3 us (8%)
  starting transfers between devices  32.4 us (5%)
  waiting for transfers between devices  15.9 us (2%)
    all_to_all x6, blocking collectives, exchange(): lax.all_to_all(rows, ('gx', 'gy'), split_axis=0, concat_axis=0, tiled=True)  99.6 us
    mul x6, other arithmetic, smooth_axis(): 0.25 * (cut(field, 0, length - 2, axis) + 2.0 * cut(field, 1, length - 1,...  96.6 us
    mul x1, other arithmetic, tensor_fields(): cross_y = smooth_all(grad_y * grad_t)  53.4 us
    reduce_sum x2, other arithmetic, solve(): curve = jnp.sum(direction * image)  45.8 us
    mul x1, other arithmetic, per_device(): flux_x = weight_x * dip_x  45.1 us
    unnamed x109, local copies, waits for them, and re-layouts  38.7 us
    dot_general x2, matrix products, forward(): return jnp.einsum('lj,kjt->klt', tables['local_y'], hat, precision=highest)  38.1 us
    dot_general x2, matrix products, backward(): jnp.einsum('ki,kjt->ijt', tables['local_x'], field, precision=highest)  29.1 us
  transfers between devices with their start and end apart: 13, of which 8 were waited for; matrix products, arithmetic and copies ran while one was open for 3% of the time, Pallas kernels for 0%

profile of v2, /device:TPU:0, one launch (start us, length us, event | category | flops | bytes accessed | tf_op | source)
XLA Modules:
  0.0 663.4 jit_solution(9006971309418705277)
XLA Ops:
  0.6 8.2 %copy.132 = f32[128,64,256]{2,0,1:T(8,128)S(1)} copy(f32[128,64,256]{2,1,0:T(8,128)} %param.11) | data formatting | bytes 16777216 | tf_op args[0]
  8.9 3.4 copy-done.6
  12.4 4.9 collective-permute-start
  17.3 1.3 collective-permute-start.1
  18.8 4.1 collective-permute-done
  22.8 4.1 collective-permute-done.1
  28.2 1.3 collective-permute-start.2
  29.5 1.5 collective-permute-start.3
  31.7 3.2 collective-permute-done.3
  34.8 3.8 pad_maximum_fusion
  38.7 3.7 copy-done.2
  42.4 4.5 slice.403
  46.9 53.4 %fusion.110 = (f32[132,68,256]{2,0,1:T(8,128)}, f32[132,68,256]{2,0,1:T(8,128)}, f32[132,68,256]{2,0,1:T(8,128)}, f32[132,68,256]{2,0,1:T(8,128)}) fusion(f32[132,68]{0,1:T(8,128)S(1)} %multiply_multiply_fusion, f32[134,70,256]{2,0,1:T(8,128)} %copy-done.2, f32[132,68,256]{2,0,1:T(8,128)} %slice.403), kind=kLoop, calls=%fused_computation.177 | loop fusion | flops 36765696 | bytes 82758720 | tf_op jit(solution)/shard_map/mul | solution.py:58
  100.4 29.5 %fusion.6 = (f32[130,68,256]{2,0,1:T(8,128)}, f32[130,68,256]{2,0,1:T(8,128)}) fusion(f32[132,68,256]{2,0,1:T(8,128)} %get-tuple-element.34, f32[132,68,256]{2,0,1:T(8,128)} %get-tuple-element.35), kind=kLoop, calls=%fused_computation.23 | loop fusion | flops 18104320 | bytes 72417280 | tf_op jit(solution)/shard_map/mul | solution.py:36
  129.9 13.7 %broadcast_multiply_fusion.4 = f32[130,66,256]{2,0,1:T(8,128)} fusion(f32[130,68,256]{2,0,1:T(8,128)} %get-tuple-element.62), kind=kLoop, calls=%fused_computation.153 | loop fusion | flops 8785920 | bytes 35143680 | tf_op jit(solution)/shard_map/mul | solution.py:36
  144.8 5.0 broadcast_multiply_fusion.5
  149.7 29.4 %fusion.2 = (f32[130,68,256]{2,0,1:T(8,128)}, f32[130,68,256]{2,0,1:T(8,128)}) fusion(f32[132,68,256]{2,0,1:T(8,128)} %get-tuple-element.32, f32[132,68,256]{2,0,1:T(8,128)} %get-tuple-element.33), kind=kLoop, calls=%fused_computation.15 | loop fusion | flops 18104320 | bytes 72417280 | tf_op jit(solution)/shard_map/mul | solution.py:36
  179.2 13.7 %broadcast_multiply_fusion.3 = f32[130,66,256]{2,0,1:T(8,128)} fusion(f32[130,68,256]{2,0,1:T(8,128)} %get-tuple-element.61), kind=kLoop, calls=%fused_computation.152 | loop fusion | flops 8785920 | bytes 35143680 | tf_op jit(solution)/shard_map/mul | solution.py:36
  194.1 5.4 broadcast_multiply_fusion.2
  199.5 1.4 slice-done.3
  202.9 45.1 %fusion.24 = (f32[130,66,256]{2,0,1:T(8,128)}, f32[130,66,256]{2,0,1:T(8,128)}, f32[130,66,256]{2,0,1:T(8,128)}, f32[130,66,256]{2,0,1:T(8,128)}) fusion(f32[130,66,256]{2,0,1:T(8,128)} %broadcast_multiply_fusion.3, f32[130,68,256]{2,0,1:T(8,128)} %get-tuple-element.61, f32[130]{0:T(256)S(1)} %and_convert_fusion.1, f32[130,68,256]{2,0,1:T(8,128)S(1)} %bitcast.166, ...), kind=kLoop, calls=%fused_computation.47 | loop fusion | flops 61501440 | bytes 140575232 | tf_op jit(solution)/shard_map/mul | solution.py:270
  248.0 26.9 %fusion.30 = (f32[130,66,256]{2,0,1:T(8,128)}, f32[130,66,256]{2,0,1:T(8,128)}) fusion(f32[130,66,256]{2,0,1:T(8,128)} %get-tuple-element.29, f32[130,66,256]{2,0,1:T(8,128)} %broadcast_multiply_fusion.2, f32[130,68,256]{2,0,1:T(8,128)} %get-tuple-element.60, f32[130,66,256]{2,0,1:T(8,128)} %get-tuple-element.28, f32[66]{0:T(128)S(1)} %copy-done.38), kind=kLoop, calls=%fused_computation.53 | loop fusion | flops 24161280 | bytes 70287624 | tf_op jit(solution)/shard_map/mul | solution.py:271
  274.8 13.4 %fusion.59 = f32[128,64,256]{2,0,1:T(8,128)S(1)} fusion(f32[130,66,256]{2,0,1:T(8,128)} %get-tuple-element.30, f32[130,66,256]{2,0,1:T(8,128)} %get-tuple-element.26), kind=kLoop, calls=%fused_computation.107 | loop fusion | flops 6291456 | bytes 41943040 | tf_op jit(solution)/shard_map/add | solution.py:272
  288.3 8.3 %fusion.153 = f32[128,64,256]{2,0,1:T(8,128)S(1)} fusion(f32[128,128,1]{1,0,2:T(8,128)S(1)} %copy-done.13, f32[128,64,256]{2,0,1:T(8,128)S(1)} %fusion.59), kind=kOutput, calls=%fused_computation.272 | convolution fusion | flops 3221225472 | bytes 16842752 | tf_op jit(solution)/shard_map/ki,ijt->kjt/dot_general | solution.py:140
  296.8 19.0 %multiply_reduce_fusion.9 = (f32[64,256]{1,0:T(8,128)S(1)}, f32[64,256]{1,0:T(8,128)S(1)}, f32[128,256]{1,0:T(8,128)S(1)}, f32[128,256]{1,0:T(8,128)S(1)}, f32[128,256,64]{1,2,0:T(8,128)}) fusion(f32[128]{0:T(128)S(1)} %copy-done.22, f32[128,64]{1,0:T(8,128)S(1)} %copy-done.16, f32[128]{0:T(128)S(1)} %copy-done.26, f32[64]{0:T(128)S(1)} %copy-done.30, ...), kind=kOutput, calls=%fused_computation.146 | convolution fusion | flops 1629388800 | bytes 17221120 | tf_op jit(solution)/shard_map/lj,kjt->klt/dot_general | solution.py:141
  316.8 24.8 %all_to_all.57 = f32[32,8,384]{2,1,0:T(8,128)S(1)} all-to-all(f32[32,8,384]{2,1,0:T(8,128)} %bitcast.179), channel_id=1, replica_groups=mesh['gx'=4,'gy'=8] {'gx','gy'}, dimensions={0} | all-to-all | bytes 786432 | tf_op jit(solution)/shard_map/all_to_all | solution.py:136
  342.5 1.7 fusion.131
  345.6 1.5 fusion.113
  347.2 1.6 fusion.135
  349.7 1.9 fusion.111
  353.8 15.6 %all_to_all.58 = f32[32,8,384]{2,1,0:T(8,128)S(1)} all-to-all(f32[32,8,384]{2,1,0:T(8,128)S(1)} %bitcast.177), channel_id=1, replica_groups=mesh['gx'=4,'gy'=8] {'gx','gy'}, dimensions={0} | all-to-all | bytes 786432 | tf_op jit(solution)/shard_map/all_to_all | solution.py:136
  372.0 1.6 copy.141
  373.6 1.6 copy.142
  375.2 13.1 %fusion.105 = f32[128,64,256]{2,1,0:T(8,128)S(1)} fusion(f32[64,64,1]{1,0,2:T(8,128)} %constant.110, f32[128,256,64]{1,2,0:T(8,128)} %get-tuple-element.58, f32[128,256]{1,0:T(8,128)S(1)} %copy.144, f32[128,256]{1,0:T(8,128)S(1)} %copy.143, f32[64,256]{1,0:T(8,128)} %copy.142, f32[64,256]{1,0:T(8,128)} %copy.141, f32[64]{0:T(128)} %constant.108, ...), kind=kOutput, calls=%fused_computation.174 | convolution fusion | flops 1629487104 | bytes 17221120 | tf_op jit(solution)/shard_map/lj,klt->kjt/dot_general | solution.py:145
  388.3 11.7 %fusion.74 = f32[128,64,256]{2,0,1:T(8,128)S(1)} fusion(f32[128,128,1]{1,0,2:T(8,128)S(1)} %copy-done.14, f32[128,64,256]{2,1,0:T(8,128)S(1)} %fusion.105), kind=kOutput, calls=%fused_computation.129 | convolution fusion | flops 3221225472 | bytes 16842752 | tf_op jit(solution)/shard_map/ki,kjt->ijt/dot_general | solution.py:146
  400.2 1.4 collective-permute-start.4
  401.6 4.5 collective-permute-start.5
  406.5 1.6 collective-permute-done.5
  408.1 1.3 collective-permute-start.6
  409.4 3.0 collective-permute-start.7
  412.5 5.4 fusion.69
  418.0 20.2 %multiply_reduce_fusion.5 = (f32[]{:T(128)}, f32[128,64,256]{2,0,1:T(8,128)}) fusion(f32[128,64,256]{2,0,1:T(8,128)S(1)} %fusion.74, f32[1,64,256]{2,0,1:T(1,128)S(1)} %collective-permute-done.4, f32[1,64,256]{2,0,1:T(1,128)S(1)} %collective-permute-done.5, f32[130,1,256]{2,0,1:T(8,128)S(1)} %collective-permute-done.7, ...), kind=kLoop, calls=%fused_computation.142 | loop fusion | flops 48234496 | bytes 50728964 | tf_op jit(solution)/shard_map/reduce_sum | solution.py:234
  439.4 11.0 %all_to_all.59 = f32[32,2,128]{2,1,0:T(2,128)S(1)} all-to-all(f32[32,2,128]{2,1,0:T(2,128)S(1)} %broadcast_in_dim.6), channel_id=1, replica_groups=mesh['gx'=4,'gy'=8] {'gx','gy'}, dimensions={0} | all-to-all | bytes 65536 | tf_op jit(solution)/shard_map/all_to_all | solution.py:136
  452.4 11.1 %fusion.108 = f32[128,64,256]{2,0,1:T(8,128)S(1)} fusion(f32[128,128,1]{1,0,2:T(8,128)S(1)} %copy-done.14, f32[128,64,256]{2,0,1:T(8,128)} %copy-done.5, f32[128,64,256]{2,0,1:T(8,128)} %get-tuple-element.25, f32[]{:T(128)} %bitcast.26), kind=kOutput, calls=%fused_computation.175 | convolution fusion | flops 3225419776 | bytes 25231364 | tf_op jit(solution)/shard_map/ki,ijt->kjt/dot_general | solution.py:140
  463.6 19.0 %multiply_reduce_fusion.4 = (f32[64,256]{1,0:T(8,128)S(1)}, f32[64,256]{1,0:T(8,128)S(1)}, f32[128,256]{1,0:T(8,128)S(1)}, f32[128,256]{1,0:T(8,128)S(1)}, f32[128,256,64]{1,2,0:T(8,128)}) fusion(f32[128]{0:T(128)S(1)} %copy-done.24, f32[128,64]{1,0:T(8,128)S(1)} %copy-done.17, f32[128]{0:T(128)S(1)} %copy-done.28, f32[64]{0:T(128)S(1)} %copy-done.32, ...), kind=kOutput, calls=%fused_computation.140 | convolution fusion | flops 1629388800 | bytes 17221120 | tf_op jit(solution)/shard_map/lj,kjt->klt/dot_general | solution.py:141
  483.6 16.1 %all_to_all.60 = f32[32,8,384]{2,1,0:T(8,128)S(1)} all-to-all(f32[32,8,384]{2,1,0:T(8,128)} %bitcast.180), channel_id=1, replica_groups=mesh['gx'=4,'gy'=8] {'gx','gy'}, dimensions={0} | all-to-all | bytes 786432 | tf_op jit(solution)/shard_map/all_to_all | solution.py:136
  502.1 1.5 fusion.114
  504.7 1.9 fusion.112
  508.9 15.5 %all_to_all.61 = f32[32,8,384]{2,1,0:T(8,128)S(1)} all-to-all(f32[32,8,384]{2,1,0:T(8,128)S(1)} %bitcast.178), channel_id=1, replica_groups=mesh['gx'=4,'gy'=8] {'gx','gy'}, dimensions={0} | all-to-all | bytes 786432 | tf_op jit(solution)/shard_map/all_to_all | solution.py:136
  524.9 7.3 %fusion.64 = f32[]{:T(128)} fusion(f32[128,256,64]{1,2,0:T(8,128)} %get-tuple-element.59, f32[128,256]{1,0:T(8,128)S(1)} %copy.158, f32[128,256]{1,0:T(8,128)S(1)} %copy.157, f32[64,256]{1,0:T(8,128)S(1)} %copy.156, f32[64,256]{1,0:T(8,128)S(1)} %copy.155, f32[64]{0:T(128)S(1)} %copy-done.37, f32[64]{0:T(128)S(1)} %copy-done.33, f32[128]{0:T(128)S(1)} %copy-done.29, ...), kind=kLoop, calls=%fused_computation.116 | loop fusion | flops 23068672 | bytes 8816132 | tf_op jit(solution)/shard_map/reduce_sum | solution.py:193
  533.4 2.6 all-to-all-start.5
  536.1 14.3 %fusion.102 = f32[128,64,256]{2,1,0:T(8,128)} fusion(f32[64,64,1]{1,0,2:T(8,128)S(1)} %copy-done.41, f32[128,256,64]{1,2,0:T(8,128)} %get-tuple-element.59, f32[128,256]{1,0:T(8,128)S(1)} %copy.158, f32[128,256]{1,0:T(8,128)S(1)} %copy.157, f32[64,256]{1,0:T(8,128)S(1)} %copy.156, f32[64,256]{1,0:T(8,128)S(1)} %copy.155, f32[64]{0:T(128)S(1)} %copy-done.37, ...), kind=kOutput, calls=%fused_computation.173 | convolution fusion | flops 1629487104 | bytes 17221120 | tf_op jit(solution)/shard_map/lj,klt->kjt/dot_general | solution.py:145
  551.2 17.4 %multiply_add_fusion.2 = f32[128,64,256]{2,0,1:T(8,128)S(1)} fusion(f32[128,64,256]{2,0,1:T(8,128)} %copy-done.3, f32[]{:T(128)} %bitcast.46, f32[128,128,1]{1,0,2:T(8,128)S(1)} %copy-done.15, f32[128,64,256]{2,1,0:T(8,128)} %fusion.102), kind=kOutput, calls=%fused_computation.136 | convolution fusion | flops 3225419776 | bytes 25231364 | tf_op jit(solution)/shard_map/ki,kjt->ijt/dot_general | solution.py:146
  568.8 1.3 collective-permute-start.8
  570.1 4.5 collective-permute-start.9
  574.9 1.6 collective-permute-done.9
  576.5 1.3 collective-permute-start.10
  577.8 3.3 collective-permute-start.11
  581.9 25.7 %multiply_reduce_fusion = (f32[]{:T(128)}, f32[128,64,256]{2,0,1:T(8,128)}) fusion(f32[128,64,256]{2,0,1:T(8,128)} %copy-done.4, f32[1,64,256]{2,0,1:T(1,128)S(1)} %collective-permute-done.8, f32[1,64,256]{2,0,1:T(1,128)S(1)} %collective-permute-done.9, f32[130,1,256]{2,0,1:T(8,128)S(1)} %collective-permute-done.11, f32[130,66,256]{2,0,1:T(8,128)S(1)} %bitcast.170, ...), kind=kLoop, calls=%fused_computation.135 | loop fusion | flops 48234496 | bytes 50728964 | tf_op jit(solution)/shard_map/reduce_sum | solution.py:234
  608.3 16.6 %all_to_all.62 = f32[32,1,128]{2,1,0:T(1,128)S(1)} all-to-all(f32[32,1,128]{2,1,0:T(1,128)S(1)} %broadcast_in_dim.8), channel_id=1, replica_groups=mesh['gx'=4,'gy'=8] {'gx','gy'}, dimensions={0} | all-to-all | bytes 32768 | tf_op jit(solution)/shard_map/all_to_all | solution.py:136
  625.0 11.8 %multiply_add_fusion.1 = f32[128,64,256]{2,0,1:T(8,128)} fusion(f32[128,64,256]{2,0,1:T(8,128)} %copy-done.4, f32[128,64,256]{2,0,1:T(8,128)} %copy-done.3, f32[]{:T(128)} %bitcast.49, f32[]{:T(128)} %bitcast.26), kind=kLoop, calls=%fused_computation.134 | loop fusion | flops 6291456 | bytes 25165832 | tf_op jit(solution)/shard_map/add | solution.py:241
  636.7 9.7 %multiply_subtract_fusion = f32[128,64,256]{2,0,1:T(8,128)S(1)} fusion(f32[128,64,256]{2,0,1:T(8,128)} %get-tuple-element.23, f32[]{:T(128)} %bitcast.49, f32[128,64,256]{2,0,1:T(8,128)} %copy-done.5, f32[128,64,256]{2,0,1:T(8,128)} %get-tuple-element.25, f32[]{:T(128)} %bitcast.26), kind=kLoop, calls=%fused_computation.133 | loop fusion | flops 8388608 | bytes 33554440 | tf_op jit(solution)/shard_map/sub | solution.py:242
  646.5 8.3 %copy.165 = f32[128,64,256]{2,1,0:T(8,128)} copy(f32[128,64,256]{2,0,1:T(8,128)S(1)} %multiply_subtract_fusion) | data formatting | bytes 16777216
  654.7 8.3 %copy.164 = f32[128,64,256]{2,1,0:T(8,128)} copy(f32[128,64,256]{2,0,1:T(8,128)S(1)} %copy-done.8) | data formatting | bytes 16777216
  (178 shorter events, 28.1 us)
Async XLA Ops:
  12.4 10.5 %collective-permute-start = (f32[3,64,256]{2,0,1:T(4,128)S(1)}, f32[3,64,256]{2,0,1:T(4,128)S(1)}, u32[]{:S(2)}, u32[]{:S(2)}) collective-permute-start(f32[3,64,256]{2,0,1:T(4,128)S(1)} %get-tuple-element.46), channel_id=1, source_target_pairs={{0,8},{8,16},{16,24},{1,9},{9,17},{17,25},{2,10},{10,18},{18,26},{... | collective-permute-start | bytes 589832 | tf_op jit(solution)/shard_map/ppermute | solution.py:22
  17.3 9.7 %collective-permute-start.1 = (f32[3,64,256]{2,0,1:T(4,128)S(1)}, f32[3,64,256]{2,0,1:T(4,128)S(1)}, u32[]{:S(2)}, u32[]{:S(2)}) collective-permute-start(f32[3,64,256]{2,0,1:T(4,128)S(1)} %get-tuple-element.47), channel_id=1, source_target_pairs={{8,0},{16,8},{24,16},{9,1},{17,9},{25,17},{10,2},{18,10},{26,18},{... | collective-permute-start | bytes 589832 | tf_op jit(solution)/shard_map/ppermute | solution.py:25
  18.7 16.2 %copy-start.7 = (f32[128,64,256]{2,0,1:T(8,128)S(1)}, f32[128,64,256]{2,0,1:T(8,128)}, u32[]{:S(2)}) copy-start(f32[128,64,256]{2,0,1:T(8,128)} %copy-done.6) | copy-start | bytes 25165828
  28.2 3.5 collective-permute-start.2
  29.5 5.4 collective-permute-start.3
  38.7 3.8 copy-start.2
  129.9 14.9 %copy-start = (f32[130,68,256]{2,0,1:T(8,128)S(1)}, f32[130,68,256]{2,0,1:T(8,128)}, u32[]{:S(2)}) copy-start(f32[130,68,256]{2,0,1:T(8,128)} %get-tuple-element.63) | copy-start | bytes 27156484
  179.2 14.9 %copy-start.1 = (f32[130,68,256]{2,0,1:T(8,128)S(1)}, f32[130,68,256]{2,0,1:T(8,128)}, u32[]{:S(2)}) copy-start(f32[130,68,256]{2,0,1:T(8,128)} %get-tuple-element.60) | copy-start | bytes 27156484
  179.2 20.3 %slice-start = ((s8[9469952]{0:T(1024)(128)(4,1)}), s8[4194304]{0:T(1024)(128)(4,1)S(1)}, s32[]{:S(2)}) async-start(s8[9469952]{0:T(1024)(128)(4,1)} %bitcast.165), calls=%async_computation.7 | async-start | bytes 8388608
  179.2 20.3 %slice-start.1 = ((s8[9469952]{0:T(1024)(128)(4,1)}), s8[4194304]{0:T(1024)(128)(4,1)S(1)}, s32[]{:S(2)}) async-start(s8[9469952]{0:T(1024)(128)(4,1)} %bitcast.165), calls=%async_computation.8 | async-start | bytes 8388608
  179.2 21.7 %slice-start.3 = ((s8[9469952]{0:T(1024)(128)(4,1)}), s8[4194304]{0:T(1024)(128)(4,1)S(1)}, s32[]{:S(2)}) async-start(s8[9469952]{0:T(1024)(128)(4,1)} %bitcast.167), calls=%async_computation.10 | async-start | bytes 8388608
  179.2 22.9 %slice-start.4 = ((s8[9469952]{0:T(1024)(128)(4,1)}), s8[4194304]{0:T(1024)(128)(4,1)S(1)}, s32[]{:S(2)}) async-start(s8[9469952]{0:T(1024)(128)(4,1)} %bitcast.167), calls=%async_computation.11 | async-start | bytes 8388608
  194.1 8.5 %slice-start.2 = ((s8[9469952]{0:T(1024)(128)(4,1)}), s8[1081344]{0:T(1024)(128)(4,1)S(1)}, s32[]{:S(2)}) async-start(s8[9469952]{0:T(1024)(128)(4,1)} %bitcast.165), calls=%async_computation.9 | async-start | bytes 2162688
  194.1 8.8 %slice-start.5 = ((s8[9469952]{0:T(1024)(128)(4,1)}), s8[1081344]{0:T(1024)(128)(4,1)S(1)}, s32[]{:S(2)}) async-start(s8[9469952]{0:T(1024)(128)(4,1)} %bitcast.167), calls=%async_computation.12 | async-start | bytes 2162688
  202.9 45.1 %copy-start.38 = (f32[66]{0:T(128)S(1)}, f32[66]{0:T(128)}, u32[]{:S(2)}) copy-start(f32[66]{0:T(128)} %and_convert_fusion) | copy-start | bytes 796
  274.8 13.4 %copy-start.13 = (f32[128,128,1]{1,0,2:T(8,128)S(1)}, f32[128,128,1]{1,0,2:T(8,128)}, u32[]{:S(2)}) copy-start(f32[128,128,1]{1,0,2:T(8,128)} %constant.109) | copy-start | bytes 196612
  288.3 8.4 %copy-start.5 = (f32[128,64,256]{2,0,1:T(8,128)}, f32[128,64,256]{2,0,1:T(8,128)S(1)}, u32[]{:S(2)}) copy-start(f32[128,64,256]{2,0,1:T(8,128)S(1)} %fusion.59) | copy-start | bytes 25165828
  288.3 8.4 %copy-start.16 = (f32[128,64]{1,0:T(8,128)S(1)}, f32[128,64]{1,0:T(8,128)}, u32[]{:S(2)}) copy-start(f32[128,64]{1,0:T(8,128)} %constant.22.clone) | copy-start | bytes 98308
  288.3 8.4 %copy-start.22 = (f32[128]{0:T(128)S(1)}, f32[128]{0:T(128)}, u32[]{:S(2)}) copy-start(f32[128]{0:T(128)} %constant.102) | copy-start | bytes 1540
  288.3 8.4 %copy-start.26 = (f32[128]{0:T(128)S(1)}, f32[128]{0:T(128)}, u32[]{:S(2)}) copy-start(f32[128]{0:T(128)} %constant.104) | copy-start | bytes 1540
  288.3 8.4 %copy-start.30 = (f32[64]{0:T(128)S(1)}, f32[64]{0:T(128)}, u32[]{:S(2)}) copy-start(f32[64]{0:T(128)} %constant.106) | copy-start | bytes 772
  288.3 8.4 %copy-start.34 = (f32[64]{0:T(128)S(1)}, f32[64]{0:T(128)}, u32[]{:S(2)}) copy-start(f32[64]{0:T(128)} %constant.108) | copy-start | bytes 772
  288.3 8.4 %copy-start.39 = (f32[64,64,1]{1,0,2:T(8,128)S(1)}, f32[64,64,1]{1,0,2:T(8,128)}, u32[]{:S(2)}) copy-start(f32[64,64,1]{1,0,2:T(8,128)} %constant.110) | copy-start | bytes 49156
  296.7 45.8 %copy-start.10 = (f32[512,512,1]{1,0,2:T(8,128)S(1)}, f32[512,512,1]{1,0,2:T(8,128)}, u32[]{:S(2)}) copy-start(f32[512,512,1]{1,0,2:T(8,128)} %constant.112) | copy-start | bytes 3145732
  296.7 47.5 %copy-start.11 = (f32[512,512,1]{1,0,2:T(8,128)S(1)}, f32[512,512,1]{1,0,2:T(8,128)}, u32[]{:S(2)}) copy-start(f32[512,512,1]{1,0,2:T(8,128)} %constant.111) | copy-start | bytes 3145732
  296.7 48.8 %copy-start.9 = (f32[512,512,1,1]{1,0,3,2:T(8,128)S(1)}, f32[512,512,1,1]{1,0,3,2:T(8,128)}, u32[]{:S(2)}) copy-start(f32[512,512,1,1]{1,0,3,2:T(8,128)} %constant.113) | copy-start | bytes 3145732
  296.8 48.8 %copy-start.19 = (f32[7,512]{1,0:T(8,128)S(1)}, f32[7,512]{1,0:T(8,128)}, u32[]{:S(2)}) copy-start(f32[7,512]{1,0:T(8,128)} %constant.71.clone) | copy-start | bytes 43012
  316.8 58.4 %copy-start.17 = (f32[128,64]{1,0:T(8,128)S(1)}, f32[128,64]{1,0:T(8,128)}, u32[]{:S(2)}) copy-start(f32[128,64]{1,0:T(8,128)} %constant.22.clone) | copy-start | bytes 98308
  375.2 13.1 %copy-start.14 = (f32[128,128,1]{1,0,2:T(8,128)S(1)}, f32[128,128,1]{1,0,2:T(8,128)}, u32[]{:S(2)}) copy-start(f32[128,128,1]{1,0,2:T(8,128)} %constant.109) | copy-start | bytes 196612
  375.2 37.2 %slice-start.9 = ((s8[8388608]{0:T(1024)(128)(4,1)}), s8[4194304]{0:T(1024)(128)(4,1)S(1)}, s32[]{:S(2)}) async-start(s8[8388608]{0:T(1024)(128)(4,1)} %bitcast.171), calls=%async_computation.16 | async-start | bytes 8388608
  388.3 24.1 %slice-start.10 = ((s8[8388608]{0:T(1024)(128)(4,1)}), s8[4194304]{0:T(1024)(128)(4,1)S(1)}, s32[]{:S(2)}) async-start(s8[8388608]{0:T(1024)(128)(4,1)} %bitcast.171), calls=%async_computation.17 | async-start | bytes 8388608
  400.0 18.0 %copy-start.3 = (f32[128,64,256]{2,0,1:T(8,128)}, f32[128,64,256]{2,0,1:T(8,128)S(1)}, u32[]{:S(2)}) copy-start(f32[128,64,256]{2,0,1:T(8,128)S(1)} %fusion.74) | copy-start | bytes 25165828
  400.0 12.4 %copy-start.20 = (f32[64,256]{1,0:T(8,128)S(1)}, f32[64,256]{1,0:T(8,128)}, u32[]{:S(2)}) copy-start(f32[64,256]{1,0:T(8,128)} %copy.141) | copy-start | bytes 196612
  400.0 12.4 %copy-start.21 = (f32[64,256]{1,0:T(8,128)S(1)}, f32[64,256]{1,0:T(8,128)}, u32[]{:S(2)}) copy-start(f32[64,256]{1,0:T(8,128)} %copy.142) | copy-start | bytes 196612
  400.0 12.4 %copy-start.23 = (f32[128]{0:T(128)S(1)}, f32[128]{0:T(128)}, u32[]{:S(2)}) copy-start(f32[128]{0:T(128)} %constant.102) | copy-start | bytes 1540
  400.0 12.4 %copy-start.27 = (f32[128]{0:T(128)S(1)}, f32[128]{0:T(128)}, u32[]{:S(2)}) copy-start(f32[128]{0:T(128)} %constant.104) | copy-start | bytes 1540
  400.1 12.4 %copy-start.31 = (f32[64]{0:T(128)S(1)}, f32[64]{0:T(128)}, u32[]{:S(2)}) copy-start(f32[64]{0:T(128)} %constant.106) | copy-start | bytes 772
  400.1 12.4 %copy-start.35 = (f32[64]{0:T(128)S(1)}, f32[64]{0:T(128)}, u32[]{:S(2)}) copy-start(f32[64]{0:T(128)} %constant.108) | copy-start | bytes 772
  400.2 6.3 collective-permute-start.4
  401.6 6.4 collective-permute-start.5
  408.1 9.9 %collective-permute-start.6 = (f32[130,1,256]{2,0,1:T(8,128)S(1)}, f32[130,1,256]{2,0,1:T(8,128)S(1)}, u32[]{:S(2)}, u32[]{:S(2)}) collective-permute-start(f32[130,1,256]{2,0,1:T(8,128)S(1)} %get-tuple-element.40), channel_id=1, source_target_pairs={{1,0},{2,1},{3,2},{4,3},{5,4},{6,5},{7,6},{9,8},{10,9},{11,10},{12... | collective-permute-start | bytes 399368 | tf_op jit(solution)/shard_map/ppermute | solution.py:25
  409.4 8.6 %collective-permute-start.7 = (f32[130,1,256]{2,0,1:T(8,128)S(1)}, f32[130,1,256]{2,0,1:T(8,128)S(1)}, u32[]{:S(2)}, u32[]{:S(2)}) collective-permute-start(f32[130,1,256]{2,0,1:T(8,128)S(1)} %get-tuple-element.41), channel_id=1, source_target_pairs={{0,1},{1,2},{2,3},{3,4},{4,5},{5,6},{6,7},{8,9},{9,10},{10,11},{11... | collective-permute-start | bytes 399368 | tf_op jit(solution)/shard_map/ppermute | solution.py:22
  452.3 11.2 %copy-start.24 = (f32[128]{0:T(128)S(1)}, f32[128]{0:T(128)}, u32[]{:S(2)}) copy-start(f32[128]{0:T(128)} %constant.102) | copy-start | bytes 1540
  452.3 11.2 %copy-start.28 = (f32[128]{0:T(128)S(1)}, f32[128]{0:T(128)}, u32[]{:S(2)}) copy-start(f32[128]{0:T(128)} %constant.104) | copy-start | bytes 1540
  452.4 11.2 %copy-start.32 = (f32[64]{0:T(128)S(1)}, f32[64]{0:T(128)}, u32[]{:S(2)}) copy-start(f32[64]{0:T(128)} %constant.106) | copy-start | bytes 772
  452.4 11.2 %copy-start.36 = (f32[64]{0:T(128)S(1)}, f32[64]{0:T(128)}, u32[]{:S(2)}) copy-start(f32[64]{0:T(128)} %constant.108) | copy-start | bytes 772
  452.4 11.2 %copy-start.40 = (f32[64,64,1]{1,0,2:T(8,128)S(1)}, f32[64,64,1]{1,0,2:T(8,128)}, u32[]{:S(2)}) copy-start(f32[64,64,1]{1,0,2:T(8,128)} %constant.110) | copy-start | bytes 49156
  483.6 41.3 %copy-start.18 = (f32[128,64]{1,0:T(8,128)S(1)}, f32[128,64]{1,0:T(8,128)}, u32[]{:S(2)}) copy-start(f32[128,64]{1,0:T(8,128)} %constant.22.clone) | copy-start | bytes 98308
  483.6 41.3 %copy-start.25 = (f32[128]{0:T(128)S(1)}, f32[128]{0:T(128)}, u32[]{:S(2)}) copy-start(f32[128]{0:T(128)} %constant.102) | copy-start | bytes 1540
  483.6 41.3 %copy-start.29 = (f32[128]{0:T(128)S(1)}, f32[128]{0:T(128)}, u32[]{:S(2)}) copy-start(f32[128]{0:T(128)} %constant.104) | copy-start | bytes 1540
  483.6 41.3 %copy-start.33 = (f32[64]{0:T(128)S(1)}, f32[64]{0:T(128)}, u32[]{:S(2)}) copy-start(f32[64]{0:T(128)} %constant.106) | copy-start | bytes 772
  483.6 41.3 %copy-start.37 = (f32[64]{0:T(128)S(1)}, f32[64]{0:T(128)}, u32[]{:S(2)}) copy-start(f32[64]{0:T(128)} %constant.108) | copy-start | bytes 772
  504.6 31.5 %copy-start.41 = (f32[64,64,1]{1,0,2:T(8,128)S(1)}, f32[64,64,1]{1,0,2:T(8,128)}, u32[]{:S(2)}) copy-start(f32[64,64,1]{1,0,2:T(8,128)} %constant.110) | copy-start | bytes 49156
  533.4 17.0 %all-to-all-start.5 = ((f32[32,1,128]{2,1,0:T(1,128)}), f32[32,1,128]{2,1,0:T(1,128)S(1)}, u32[]{:S(2)}, u32[]{:S(2)}) async-start(f32[32,1,128]{2,1,0:T(1,128)} %broadcast_in_dim.7), calls=%async_computation.5 | async-start | bytes 32768 | tf_op jit(solution)/shard_map/all_to_all | solution.py:136
  536.1 15.1 %copy-start.15 = (f32[128,128,1]{1,0,2:T(8,128)S(1)}, f32[128,128,1]{1,0,2:T(8,128)}, u32[]{:S(2)}) copy-start(f32[128,128,1]{1,0,2:T(8,128)} %constant.109) | copy-start | bytes 196612
  551.2 30.7 %slice-start.6 = ((s8[9191424]{0:T(1024)(128)(4,1)}), s8[4194304]{0:T(1024)(128)(4,1)S(1)}, s32[]{:S(2)}) async-start(s8[9191424]{0:T(1024)(128)(4,1)} %bitcast.169), calls=%async_computation.13 | async-start | bytes 8388608
  551.2 30.7 %slice-start.7 = ((s8[9191424]{0:T(1024)(128)(4,1)}), s8[4194304]{0:T(1024)(128)(4,1)S(1)}, s32[]{:S(2)}) async-start(s8[9191424]{0:T(1024)(128)(4,1)} %bitcast.169), calls=%async_computation.14 | async-start | bytes 8388608
  551.2 30.7 %slice-start.8 = ((s8[9191424]{0:T(1024)(128)(4,1)}), s8[802816]{0:T(1024)(128)(4,1)S(1)}, s32[]{:S(2)}) async-start(s8[9191424]{0:T(1024)(128)(4,1)} %bitcast.169), calls=%async_computation.15 | async-start | bytes 1605632
  568.7 7.9 %copy-start.4 = (f32[128,64,256]{2,0,1:T(8,128)}, f32[128,64,256]{2,0,1:T(8,128)S(1)}, u32[]{:S(2)}) copy-start(f32[128,64,256]{2,0,1:T(8,128)S(1)} %multiply_add_fusion.2) | copy-start | bytes 25165828
  568.8 6.2 collective-permute-start.8
  570.1 6.4 collective-permute-start.9
  576.5 4.6 collective-permute-start.10
  577.8 4.0 collective-permute-start.11
  646.4 8.3 %copy-start.8 = (f32[128,64,256]{2,0,1:T(8,128)S(1)}, f32[128,64,256]{2,0,1:T(8,128)}, u32[]{:S(2)}) copy-start(f32[128,64,256]{2,0,1:T(8,128)} %multiply_add_fusion.1) | copy-start | bytes 25165828
  (2 other events, 4.1 us)
